TPU v7x, 128 devices: a whole 4x4x4 slice. The times are simulated.
128 devices in a mesh: gx: 16 (over y, z), gy: 8 (over x, core).
Axes of the slice: x: 4, y: 4, z: 4, core: 2. Of those that a mesh axis runs over, the one named last changes fastest.
Arguments:
- probes: bfloat16 [16, 131072], P(None, ('gx', 'gy')), may hold values from -73 to 73, as said below
- previous: bfloat16 [16, 131072], P(None, ('gx', 'gy')), may hold values from -6 to 6
- prev_coupling: float32 [16, 16], replicated, may hold values from -1.5 to 1.5
- leaves: bfloat16 [128, 1024, 1024], P(('gx', 'gy')), may hold values from -1 to 3, as said below
- bases: bfloat16 [7, 64, 131072], P(None, None, ('gx', 'gy')), may hold values from -6 to 6
- leaf_sizes: int32 [128], P(('gx', 'gy')), may hold values from 1 to 1024, 98304 in all
Outputs:
- rayleigh: float32 [16, 16], replicated
- factor: float32 [16, 16], replicated
- next_block: float32 [16, 131072], P(None, ('gx', 'gy'))
Inputs may be any that keep to these rules, and one draw needn't show every extreme that they name: For every probe p and slot s, |probes[p, s]| stays within the range below. Each leaves[i] is symmetric. `leaf_sizes`: the real points of a leaf fill its first slots; the sizes sum to 98304.
All inputs are finite; a program needn't handle non-finite values. No bound on the sum of `leaf_sizes` on one device may be relied on, other than what follows from the above.
Results may differ from a plain program's by a relative error of at most 0.0022.
Values sent between devices are 32-bit elements; how exact they have to be, the bound alone decides.
No kernel may reach another device: no remote copies, remote signals or barrier semaphores. Data moves between devices by JAX's collectives and lax.ppermute only.
A program may use at most 64 MiB of HBM per device.

v0:
```python
import math

import jax
import jax.numpy as jnp
from jax import lax
from jax.sharding import Mesh
from jax.sharding import PartitionSpec as P

GX_GY = ("gx_0", "gx_1", "gy_0", "gy_1")


def partner_2(block, axis, stride):
    count = lax.axis_size(axis)
    route = []
    for low in range(count):
        high = low | 1 << stride
        if high != low and high < count:
            route += [(low, high), (high, low)]
    return lax.ppermute(block, axis, route)


def one_axis_at_a_time(value, axes):
    for axis in axes:
        value = lax.psum(value, axis)
    return value


def sibling_sums(partials, spread):
    results = []
    remaining = partials
    for bit_number in range(spread):
        received = partner_2(remaining, GX_GY, bit_number)
        results.append(received[0])
        remaining = remaining[1:] + received[1:]
    return results


def body(probes, previous, prev_coupling, leaves, bases, leaf_sizes):
    highest = lax.Precision.HIGHEST
    probe_count = probes.shape[0]
    leaf_count = leaves.shape[0]
    leaf_rows = leaves.shape[1]
    rows = leaf_count * leaf_rows
    rank = bases.shape[1]
    devices = lax.axis_size(GX_GY)
    spread = devices.bit_length() - 1
    filled = leaf_count * devices * leaf_rows * 3 // 4
    inverse = 1.0 / filled
    valid = (jnp.arange(leaf_rows, dtype=jnp.int32)[None, :] < leaf_sizes[:, None]).reshape(rows)
    block = jnp.where(valid[None, :], probes, jnp.zeros_like(probes))
    older = jnp.where(valid[None, :], previous, jnp.zeros_like(previous))
    shaped = block.reshape(probe_count, leaf_count, leaf_rows)
    image = jnp.einsum("lrc,plc->plr", leaves, shaped, preferred_element_type=jnp.float32).reshape(
        probe_count, rows
    )
    partials = jnp.einsum("pm,krm->kpr", block, bases, preferred_element_type=jnp.float32)
    partners = sibling_sums(partials, spread)
    for bit_number in range(spread):
        width = rows * 2**bit_number
        scaled = (partners[bit_number] * (1.0 / math.sqrt(rank * width))).astype(jnp.bfloat16)
        image = image + jnp.dot(scaled, bases[bit_number], preferred_element_type=jnp.float32)
    image = jnp.where(valid[None, :], image, jnp.zeros_like(image))
    dense = block.astype(jnp.float32)
    older_dense = older.astype(jnp.float32)
    stacked = jnp.concatenate([image, dense, older_dense], 0)
    joint = one_axis_at_a_time(jnp.dot(stacked, stacked.T, precision=highest) * inverse, GX_GY)
    rayleigh = joint[probe_count : 2 * probe_count, :probe_count]
    mixing = jnp.concatenate(
        [jnp.eye(probe_count, dtype=jnp.float32), -rayleigh.T, -prev_coupling], 1
    )
    gram = jnp.dot(jnp.dot(mixing, joint, precision=highest), mixing.T, precision=highest)
    residual = (
        image
        - jnp.dot(rayleigh.T, dense, precision=highest)
        - jnp.dot(prev_coupling, older_dense, precision=highest)
    )
    factor = jnp.linalg.cholesky(gram)
    next_block = jax.scipy.linalg.solve_triangular(factor, residual, lower=True)
    return (rayleigh, factor, next_block)


def solution(mesh):
    split = Mesh(mesh.devices.reshape(4, 4, 4, 2), ("gx_0", "gx_1", "gy_0", "gy_1"))
    return jax.shard_map(
        body,
        mesh=split,
        in_specs=(
            P(None, GX_GY),
            P(None, GX_GY),
            P(),
            P(GX_GY, None, None),
            P(None, None, GX_GY),
            P(GX_GY),
        ),
        out_specs=(P(), P(), P(None, GX_GY)),
        check_vma=False,
    )
```

profile of v0, /device:TPU:0, one launch (start us, length us, event | category | flops | bytes accessed | tf_op | source)
XLA Modules:
  0.0 96.4 jit_solution(13078462689037245916)
XLA Ops:
  1.5 1.7 %convolution_bitcast_fusion.1 = f32[7,16,64]{2,1,0:T(8,128)S(1)} fusion(bf16[7,64,1024]{2,1,0:T(8,128)(2,1)} %param.10, bf16[16,1024]{1,0:T(8,128)(2,1)} %param.6, pred[1024]{0:T(1024)(128)(4,1)S(1)} %iota_compare_fusion.2), kind=kOutput, calls=%fused_computation.13 | convolution fusion | flops 14696448 | bytes 979968 | tf_op jit(solution)/shard_map/pm,krm->kpr/dot_general | solution.py:56
  3.3 1.4 %fusion = f32[16,1024]{1,0:T(8,128)S(1)} fusion(bf16[1,1024,1024]{2,1,0:T(8,128)(2,1)S(1)} %copy-done, bf16[16,1024]{1,0:T(8,128)(2,1)} %param.6, pred[1024]{0:T(1024)(128)(4,1)S(1)} %iota_compare_fusion.2), kind=kOutput, calls=%fused_computation | convolution fusion | flops 33570816 | bytes 2196480 | tf_op jit(solution)/shard_map/lrc,plc->plr/dot_general | solution.py:53
  4.8 1.7 %collective-permute-start.1 = (f32[6,16,64]{2,1,0:T(8,128)S(1)}, f32[6,16,64]{2,1,0:T(8,128)S(1)}, u32[]{:S(2)}, u32[]{:S(2)}) collective-permute-start(f32[6,16,64]{2,1,0:T(8,128)S(1)} %slice_add_fusion), channel_id=1, source_target_pairs={{0,2},{2,0},{1,3},{3,1},{4,6},{6,4},{5,7},{7,5},{8,10},{10,8},{9,1... | collective-permute-start | bytes 73736 | tf_op jit(solution)/shard_map/ppermute | solution.py:19
  6.6 2.4 %collective-permute-done.1 = f32[6,16,64]{2,1,0:T(8,128)S(1)} collective-permute-done((f32[6,16,64]{2,1,0:T(8,128)S(1)}, f32[6,16,64]{2,1,0:T(8,128)S(1)}, u32[]{:S(2)}, u32[]{:S(2)}) %collective-permute-start.1) | collective-permute-done | bytes 24608 | tf_op jit(solution)/shard_map/ppermute | solution.py:19
  9.0 3.1 %collective-permute-start.2 = (f32[5,16,64]{2,1,0:T(8,128)S(1)}, f32[5,16,64]{2,1,0:T(8,128)S(1)}, u32[]{:S(2)}, u32[]{:S(2)}) collective-permute-start(f32[5,16,64]{2,1,0:T(8,128)S(1)} %slice_add_fusion.1), channel_id=1, source_target_pairs={{0,4},{4,0},{1,5},{5,1},{2,6},{6,2},{3,7},{7,3},{8,12},{12,8},{9,1... | collective-permute-start | bytes 61448 | tf_op jit(solution)/shard_map/ppermute | solution.py:19
  12.3 2.3 %collective-permute-done.2 = f32[5,16,64]{2,1,0:T(8,128)S(1)} collective-permute-done((f32[5,16,64]{2,1,0:T(8,128)S(1)}, f32[5,16,64]{2,1,0:T(8,128)S(1)}, u32[]{:S(2)}, u32[]{:S(2)}) %collective-permute-start.2) | collective-permute-done | bytes 20512 | tf_op jit(solution)/shard_map/ppermute | solution.py:19
  14.5 2.0 %collective-permute-start.3 = (f32[4,16,64]{2,1,0:T(8,128)S(1)}, f32[4,16,64]{2,1,0:T(8,128)S(1)}, u32[]{:S(2)}, u32[]{:S(2)}) collective-permute-start(f32[4,16,64]{2,1,0:T(8,128)S(1)} %slice_add_fusion.2), channel_id=1, source_target_pairs={{0,8},{8,0},{1,9},{9,1},{2,10},{10,2},{3,11},{11,3},{4,12},{12,4},... | collective-permute-start | bytes 49160 | tf_op jit(solution)/shard_map/ppermute | solution.py:19
  16.7 1.8 %collective-permute-done.3 = f32[4,16,64]{2,1,0:T(8,128)S(1)} collective-permute-done((f32[4,16,64]{2,1,0:T(8,128)S(1)}, f32[4,16,64]{2,1,0:T(8,128)S(1)}, u32[]{:S(2)}, u32[]{:S(2)}) %collective-permute-start.3) | collective-permute-done | bytes 16416 | tf_op jit(solution)/shard_map/ppermute | solution.py:19
  18.5 4.0 %collective-permute-start.4 = (f32[3,16,64]{2,1,0:T(8,128)S(1)}, f32[3,16,64]{2,1,0:T(8,128)S(1)}, u32[]{:S(2)}, u32[]{:S(2)}) collective-permute-start(f32[3,16,64]{2,1,0:T(8,128)S(1)} %slice_add_fusion.3), channel_id=1, source_target_pairs={{0,16},{16,0},{1,17},{17,1},{2,18},{18,2},{3,19},{19,3},{4,20},{20... | collective-permute-start | bytes 36872 | tf_op jit(solution)/shard_map/ppermute | solution.py:19
  22.6 1.7 %collective-permute-done.4 = f32[3,16,64]{2,1,0:T(8,128)S(1)} collective-permute-done((f32[3,16,64]{2,1,0:T(8,128)S(1)}, f32[3,16,64]{2,1,0:T(8,128)S(1)}, u32[]{:S(2)}, u32[]{:S(2)}) %collective-permute-start.4) | collective-permute-done | bytes 12320 | tf_op jit(solution)/shard_map/ppermute | solution.py:19
  24.2 1.6 %collective-permute-start.5 = (f32[2,16,64]{2,1,0:T(8,128)S(1)}, f32[2,16,64]{2,1,0:T(8,128)S(1)}, u32[]{:S(2)}, u32[]{:S(2)}) collective-permute-start(f32[2,16,64]{2,1,0:T(8,128)S(1)} %slice_add_fusion.4), channel_id=1, source_target_pairs={{0,32},{32,0},{1,33},{33,1},{2,34},{34,2},{3,35},{35,3},{4,36},{36... | collective-permute-start | bytes 24584 | tf_op jit(solution)/shard_map/ppermute | solution.py:19
  25.9 2.0 %collective-permute-done.5 = f32[2,16,64]{2,1,0:T(8,128)S(1)} collective-permute-done((f32[2,16,64]{2,1,0:T(8,128)S(1)}, f32[2,16,64]{2,1,0:T(8,128)S(1)}, u32[]{:S(2)}, u32[]{:S(2)}) %collective-permute-start.5) | collective-permute-done | bytes 8224 | tf_op jit(solution)/shard_map/ppermute | solution.py:19
  28.0 3.2 %collective-permute-start.6 = (f32[1,16,64]{2,1,0:T(8,128)S(1)}, f32[1,16,64]{2,1,0:T(8,128)S(1)}, u32[]{:S(2)}, u32[]{:S(2)}) collective-permute-start(f32[1,16,64]{2,1,0:T(8,128)S(1)} %slice_add_fusion.5), channel_id=1, source_target_pairs={{0,64},{64,0},{1,65},{65,1},{2,66},{66,2},{3,67},{67,3},{4,68},{68... | collective-permute-start | bytes 12296 | tf_op jit(solution)/shard_map/ppermute | solution.py:19
  31.3 1.8 %collective-permute-done.6 = f32[1,16,64]{2,1,0:T(8,128)S(1)} collective-permute-done((f32[1,16,64]{2,1,0:T(8,128)S(1)}, f32[1,16,64]{2,1,0:T(8,128)S(1)}, u32[]{:S(2)}, u32[]{:S(2)}) %collective-permute-start.6) | collective-permute-done | bytes 4128 | tf_op jit(solution)/shard_map/ppermute | solution.py:19
  33.6 17.3 %psum.28 = f32[48,48]{0,1:T(8,128)S(1)} all-reduce(f32[48,48]{0,1:T(8,128)S(1)} %convolution_multiply_fusion), channel_id=1, replica_groups=mesh['gx_0'=4,'gx_1'=4,'gy_0'=4,'gy_1'=2] {'gx_0'}, use_global_device_ids=true, to_apply=%region_0.1 | all-reduce | flops 2304 | bytes 18432 | tf_op jit(solution)/shard_map/psum | solution.py:24
  50.9 18.0 %psum.29 = f32[48,48]{0,1:T(8,128)S(1)} all-reduce(f32[48,48]{0,1:T(8,128)S(1)} %psum.28), channel_id=1, replica_groups=mesh['gx_0'=4,'gx_1'=4,'gy_0'=4,'gy_1'=2] {'gx_1'}, use_global_device_ids=true, to_apply=%region_1.2 | all-reduce | flops 2304 | bytes 18432 | tf_op jit(solution)/shard_map/psum | solution.py:24
  68.8 17.0 %psum.30 = f32[48,48]{0,1:T(8,128)S(1)} all-reduce(f32[48,48]{0,1:T(8,128)S(1)} %psum.29), channel_id=1, replica_groups=mesh['gx_0'=4,'gx_1'=4,'gy_0'=4,'gy_1'=2] {'gy_0'}, use_global_device_ids=true, to_apply=%region_2.3 | all-reduce | flops 2304 | bytes 18432 | tf_op jit(solution)/shard_map/psum | solution.py:24
  85.9 3.4 %psum.31 = f32[48,48]{0,1:T(8,128)S(1)} all-reduce(f32[48,48]{0,1:T(8,128)S(1)} %psum.30), channel_id=1, replica_groups=mesh['gx_0'=4,'gx_1'=4,'gy_0'=4,'gy_1'=2] {'gy_1'}, use_global_device_ids=true, to_apply=%region_3.4 | all-reduce | flops 2304 | bytes 18432 | tf_op jit(solution)/shard_map/psum | solution.py:24
  90.2 0.7 copy.11
  90.9 1.5 %cholesky.20 = f32[16,16]{1,0:T(8,128)S(1)} custom-call(f32[16,16]{1,0:T(8,128)S(1)} %fusion.38), custom_call_target="Cholesky" | custom-call | tf_op jit(solution)/shard_map/jit(cholesky)/cholesky | solution.py:77
  92.4 0.6 compare_reduce_fusion
  93.1 1.2 %select_bitcast_fusion = (f32[1,16,16]{2,1,0:T(8,128)S(1)}, f32[16,16]{1,0:T(8,128)}) fusion(f32[16,16]{1,0:T(8,128)S(1)} %cholesky.20, pred[]{:T(512)} %compare_reduce_fusion), kind=kLoop, calls=%fused_computation.66 | loop fusion | flops 1024 | bytes 3073 | tf_op jit(solution)/shard_map/jit(_solve_triangular)/triangular_solve | solution.py:78
  94.3 1.2 %custom-call.7 = f32[1,16,16]{1,2,0:T(8,128)S(1)} custom-call(f32[1,16,16]{2,1,0:T(8,128)S(1)} %get-tuple-element.6), custom_call_target="InvertDiagBlocksLowerTriangular" | custom-call | tf_op jit(solution)/shard_map/jit(_solve_triangular)/triangular_solve | solution.py:78
  95.5 0.9 fusion.36
  (38 shorter events, 2.4 us)
Async XLA Ops:
  0.6 2.6 %copy-start = (bf16[1,1024,1024]{2,1,0:T(8,128)(2,1)S(1)}, bf16[1,1024,1024]{2,1,0:T(8,128)(2,1)}, u32[]{:S(2)}) copy-start(bf16[1,1024,1024]{2,1,0:T(8,128)(2,1)} %param.9) | copy-start | bytes 6291460
  0.6 5.8 %copy-start.1 = (bf16[7,64,1024]{2,1,0:T(8,128)(2,1)S(1)}, bf16[7,64,1024]{2,1,0:T(8,128)(2,1)}, u32[]{:S(2)}) copy-start(bf16[7,64,1024]{2,1,0:T(8,128)(2,1)} %param.10) | copy-start | bytes 2752516
  0.7 4.0 %copy-start.2 = (bf16[16,1024]{1,0:T(8,128)(2,1)S(1)}, bf16[16,1024]{1,0:T(8,128)(2,1)}, u32[]{:S(2)}) copy-start(bf16[16,1024]{1,0:T(8,128)(2,1)} %param.6) | copy-start | bytes 98308
  0.7 4.0 %copy-start.3 = (bf16[16,1024]{1,0:T(8,128)(2,1)S(1)}, bf16[16,1024]{1,0:T(8,128)(2,1)}, u32[]{:S(2)}) copy-start(bf16[16,1024]{1,0:T(8,128)(2,1)} %param.7) | copy-start | bytes 98308
  0.7 4.1 %copy-start.4 = (f32[16,16]{1,0:T(8,128)S(1)}, f32[16,16]{1,0:T(8,128)}, u32[]{:S(2)}) copy-start(f32[16,16]{1,0:T(8,128)} %param.8) | copy-start | bytes 3076
  3.2 1.5 %collective-permute-start = (f32[7,16,64]{2,1,0:T(8,128)S(1)}, f32[7,16,64]{2,1,0:T(8,128)S(1)}, u32[]{:S(2)}, u32[]{:S(2)}) collective-permute-start(f32[7,16,64]{2,1,0:T(8,128)S(1)} %convolution_bitcast_fusion.1), channel_id=1, source_target_pairs={{0,1},{1,0},{2,3},{3,2},{4,5},{5,4},{6,7},{7,6},{8,9},{9,8},{10,11... | collective-permute-start | bytes 86024 | tf_op jit(solution)/shard_map/ppermute | solution.py:19
  4.8 4.2 %collective-permute-start.1 = (f32[6,16,64]{2,1,0:T(8,128)S(1)}, f32[6,16,64]{2,1,0:T(8,128)S(1)}, u32[]{:S(2)}, u32[]{:S(2)}) collective-permute-start(f32[6,16,64]{2,1,0:T(8,128)S(1)} %slice_add_fusion), channel_id=1, source_target_pairs={{0,2},{2,0},{1,3},{3,1},{4,6},{6,4},{5,7},{7,5},{8,10},{10,8},{9,1... | collective-permute-start | bytes 73736 | tf_op jit(solution)/shard_map/ppermute | solution.py:19
  9.0 5.5 %collective-permute-start.2 = (f32[5,16,64]{2,1,0:T(8,128)S(1)}, f32[5,16,64]{2,1,0:T(8,128)S(1)}, u32[]{:S(2)}, u32[]{:S(2)}) collective-permute-start(f32[5,16,64]{2,1,0:T(8,128)S(1)} %slice_add_fusion.1), channel_id=1, source_target_pairs={{0,4},{4,0},{1,5},{5,1},{2,6},{6,2},{3,7},{7,3},{8,12},{12,8},{9,1... | collective-permute-start | bytes 61448 | tf_op jit(solution)/shard_map/ppermute | solution.py:19
  14.5 3.9 %collective-permute-start.3 = (f32[4,16,64]{2,1,0:T(8,128)S(1)}, f32[4,16,64]{2,1,0:T(8,128)S(1)}, u32[]{:S(2)}, u32[]{:S(2)}) collective-permute-start(f32[4,16,64]{2,1,0:T(8,128)S(1)} %slice_add_fusion.2), channel_id=1, source_target_pairs={{0,8},{8,0},{1,9},{9,1},{2,10},{10,2},{3,11},{11,3},{4,12},{12,4},... | collective-permute-start | bytes 49160 | tf_op jit(solution)/shard_map/ppermute | solution.py:19
  18.5 5.8 %collective-permute-start.4 = (f32[3,16,64]{2,1,0:T(8,128)S(1)}, f32[3,16,64]{2,1,0:T(8,128)S(1)}, u32[]{:S(2)}, u32[]{:S(2)}) collective-permute-start(f32[3,16,64]{2,1,0:T(8,128)S(1)} %slice_add_fusion.3), channel_id=1, source_target_pairs={{0,16},{16,0},{1,17},{17,1},{2,18},{18,2},{3,19},{19,3},{4,20},{20... | collective-permute-start | bytes 36872 | tf_op jit(solution)/shard_map/ppermute | solution.py:19
  24.2 3.7 %collective-permute-start.5 = (f32[2,16,64]{2,1,0:T(8,128)S(1)}, f32[2,16,64]{2,1,0:T(8,128)S(1)}, u32[]{:S(2)}, u32[]{:S(2)}) collective-permute-start(f32[2,16,64]{2,1,0:T(8,128)S(1)} %slice_add_fusion.4), channel_id=1, source_target_pairs={{0,32},{32,0},{1,33},{33,1},{2,34},{34,2},{3,35},{35,3},{4,36},{36... | collective-permute-start | bytes 24584 | tf_op jit(solution)/shard_map/ppermute | solution.py:19
  28.0 5.2 %collective-permute-start.6 = (f32[1,16,64]{2,1,0:T(8,128)S(1)}, f32[1,16,64]{2,1,0:T(8,128)S(1)}, u32[]{:S(2)}, u32[]{:S(2)}) collective-permute-start(f32[1,16,64]{2,1,0:T(8,128)S(1)} %slice_add_fusion.5), channel_id=1, source_target_pairs={{0,64},{64,0},{1,65},{65,1},{2,66},{66,2},{3,67},{67,3},{4,68},{68... | collective-permute-start | bytes 12296 | tf_op jit(solution)/shard_map/ppermute | solution.py:19
where the time goes:
time: 98 us; the launch traced here: 96.4 us
  blocking collectives  55.7 us (57%)
  starting transfers between devices  15.5 us (16%)
  waiting for transfers between devices  12 us (12%)
  matrix products  6.12 us (6%)
  other arithmetic  4.75 us (5%)
  between operations  1.6 us (2%)
    psum x4, blocking collectives, one_axis_at_a_time(): value = lax.psum(value, axis)  55.7 us
    ppermute x7, starting transfers between devices, partner_2(): return lax.ppermute(block, axis, route)  15.5 us
    ppermute x7, waiting for transfers between devices, partner_2(): return lax.ppermute(block, axis, route)  12 us
    another operation x2, other arithmetic, body(): next_block = jax.scipy.linalg.solve_triangular(factor, residual, lower=True)  2.47 us
    another operation x3, other arithmetic, body(): factor = jnp.linalg.cholesky(gram)  2.13 us
  transfers between devices with their start and end apart: 7, of which 6 were waited for; matrix products, arithmetic and copies ran while one was open for 2% of the time, Pallas kernels for 0%

commit v1 on v0

v1 whole, which is shorter than its diff:
```python
import math

import jax
import jax.numpy as jnp
from jax import lax
from jax.sharding import Mesh
from jax.sharding import PartitionSpec as P

AXES = ("gx_0", "gx_1", "gy_0", "gy_1")
CHIPS = ("gx_0", "gx_1", "gy_0")
CORE = "gy_1"
HIGHEST = lax.Precision.HIGHEST


def fold(m):
    half = m.shape[-2] // 2
    return jnp.concatenate([m[..., :half, :], m[..., half:, :]], -1)


def unfold(m):
    half = m.shape[-1] // 2
    return jnp.concatenate([m[..., :half], m[..., half:]], -2)


def body(probes, previous, prev_coupling, leaves, bases, leaf_sizes):
    probe_count = probes.shape[0]
    rows = leaves.shape[1]
    rank = bases.shape[1]
    levels = bases.shape[0]
    chips = lax.axis_size(CHIPS)
    chip_bits = chips.bit_length() - 1
    devices = lax.axis_size(AXES)
    inverse = 1.0 / (devices * rows * 3 // 4)
    chip = lax.axis_index(CHIPS)
    valid = (jnp.arange(rows, dtype=jnp.int32) < leaf_sizes[0])[None, :]
    block = jnp.where(valid, probes, jnp.zeros_like(probes))
    older = jnp.where(valid, previous, jnp.zeros_like(previous))
    partials = jnp.einsum("pm,krm->kpr", block, bases, preferred_element_type=jnp.float32)
    partials = fold(partials)
    other = lax.ppermute(partials, CORE, [(0, 1), (1, 0)])
    image = jnp.einsum("rc,pc->pr", leaves[0], block, preferred_element_type=jnp.float32)
    mine = partials + other
    send = jnp.zeros((chips,) + mine.shape[1:], jnp.float32)
    apart = chip ^ jnp.arange(chips, dtype=jnp.int32)
    for bit in range(chip_bits):
        here = ((apart >> bit) == 1)[:, None, None]
        send = jnp.where(here, mine[bit + 1][None], send)
    got = lax.all_to_all(send, CHIPS, 0, 0, tiled=True)
    partners = [other[0]]
    for bit in range(chip_bits):
        first = ((chip >> bit) ^ 1) << bit
        partners.append(lax.dynamic_slice_in_dim(got, first, 1 << bit, 0).sum(0))
    scaled = [
        unfold(partners[level] * (1.0 / math.sqrt(rank * rows * 2**level))).astype(jnp.bfloat16)
        for level in range(levels)
    ]
    image = image + jnp.einsum(
        "kpr,krm->pm", jnp.stack(scaled), bases, preferred_element_type=jnp.float32
    )
    image = jnp.where(valid, image, jnp.zeros_like(image))
    dense = block.astype(jnp.float32)
    shifted = image - jnp.dot(prev_coupling, older.astype(jnp.float32), precision=HIGHEST)
    left = jnp.concatenate([shifted, dense], 0)
    right = jnp.concatenate([shifted, dense, image], 0)
    sums = jnp.dot(left, right.T, precision=HIGHEST)
    p = probe_count
    packed = jnp.concatenate(
        [sums[:p, :p], sums[p:, :p], sums[p:, p : 2 * p], sums[p:, 2 * p :]], 1
    )
    packed = fold(packed)
    packed = packed + lax.ppermute(packed, CORE, [(0, 1), (1, 0)])
    spread = jnp.broadcast_to(packed[None], (chips,) + packed.shape)
    total = unfold(lax.all_to_all(spread, CHIPS, 0, 0, tiled=True).sum(0)) * inverse
    shifted_shifted, block_shifted, block_block, rayleigh = jnp.split(total, 4, 1)
    cross = jnp.dot(rayleigh.T, block_shifted, precision=HIGHEST)
    inner = jnp.dot(rayleigh.T, block_block, precision=HIGHEST)
    gram = shifted_shifted - cross - cross.T + jnp.dot(inner, rayleigh, precision=HIGHEST)
    residual = shifted - jnp.dot(rayleigh.T, dense, precision=HIGHEST)
    factor = jnp.linalg.cholesky(gram)
    next_block = jax.scipy.linalg.solve_triangular(factor, residual, lower=True)
    return (rayleigh, factor, next_block)


def solution(mesh):
    split = Mesh(mesh.devices.reshape(4, 4, 4, 2), AXES)
    return jax.shard_map(
        body,
        mesh=split,
        in_specs=(
            P(None, AXES),
            P(None, AXES),
            P(),
            P(AXES, None, None),
            P(None, None, AXES),
            P(AXES),
        ),
        out_specs=(P(), P(), P(None, AXES)),
        check_vma=False,
    )
```

time: 98 us -> 55 us (0.56); the launches traced: 96.4 us -> 54.7 us
  blocking collectives: 55.7 us -> 15.6 us
  starting transfers between devices: 15.5 us -> 11.7 us
  other arithmetic: 4.75 us -> 7.29 us
  matrix products: 6.12 us -> 4.53 us
    psum x4 -> x0, blocking collectives: 55.7 us -> none  [one_axis_at_a_time(): value = lax.psum(value, axis)]
    all_to_all x0 -> x1, blocking collectives: none -> 15.6 us  [body(): lax.all_to_all(spread, CHIPS, 0, 0, tiled=True).sum(0)]
    ppermute x7 -> x2, starting transfers between devices: 15.5 us -> 0.05 us  [the longest x1 0.03 us: body(): other = lax.ppermute(partials, CORE, [(0, 1), (1, 0)])]
    all_to_all x0 -> x1, starting transfers between devices: none -> 11.6 us  [body(): got = lax.all_to_all(send, CHIPS, 0, 0, tiled=True)]
    all_to_all x0 -> x1, waiting for transfers between devices: none -> 10.8 us  [body(): got = lax.all_to_all(send, CHIPS, 0, 0, tiled=True)]
    ppermute x7 -> x2, waiting for transfers between devices: 12 us -> 1.47 us  [the longest x1 1.15 us: body(): packed = packed + lax.ppermute(packed, CORE, [(0, 1), (1, 0)])]
    dot_general x13 -> x8, matrix products: 3.47 us -> 1.92 us  [the longest x1 0.65 us: body(): jnp.einsum('rc,pc->pr', leaves[0], block, preferred_element_type=jnp.floa...]
    select_n x0 -> x1, other arithmetic: none -> 1.26 us  [body(): send = jnp.where(here, mine[bit + 1][None], send)]
  transfers between devices with their start and end apart: 7 -> 3, of which waited for: 6 -> 3; matrix products, arithmetic and copies ran while one was open for 2% -> 2% of each run, Pallas kernels for 0% -> 0%
where the time goes in v1:
time: 55 us; the launch traced here: 54.7 us
  blocking collectives  15.6 us (28%)
  waiting for transfers between devices  12.3 us (22%)
  starting transfers between devices  11.7 us (21%)
  other arithmetic  7.29 us (13%)
  matrix products  4.53 us (8%)
  between operations  1.67 us (3%)
  local copies, waits for them, and re-layouts  1.61 us (3%)
    all_to_all x1, blocking collectives, body(): lax.all_to_all(spread, CHIPS, 0, 0, tiled=True).sum(0)  15.6 us
    all_to_all x1, starting transfers between devices, body(): got = lax.all_to_all(send, CHIPS, 0, 0, tiled=True)  11.6 us
    all_to_all x1, waiting for transfers between devices, body(): got = lax.all_to_all(send, CHIPS, 0, 0, tiled=True)  10.8 us
    another operation x2, other arithmetic, body(): next_block = jax.scipy.linalg.solve_triangular(factor, residual, lower=True)  2.47 us
    another operation x3, other arithmetic, body(): factor = jnp.linalg.cholesky(gram)  2.14 us
    dot_general x1, matrix products, body(): jnp.einsum('pm,krm->kpr', block, bases, preferred_element_type=jnp.float32)  1.72 us
    select_n x1, other arithmetic, body(): send = jnp.where(here, mine[bit + 1][None], send)  1.26 us
    ppermute x1, waiting for transfers between devices, body(): packed = packed + lax.ppermute(packed, CORE, [(0, 1), (1, 0)])  1.15 us
  transfers between devices with their start and end apart: 3, of which 3 were waited for; matrix products, arithmetic and copies ran while one was open for 2% of the time, Pallas kernels for 0%

profile of v1, /device:TPU:0, one launch (start us, length us, event | category | flops | bytes accessed | tf_op | source)
XLA Modules:
  0.0 54.7 jit_solution(16748553339485683815)
XLA Ops:
  1.5 1.7 %convolution_bitcast_fusion.2 = f32[7,16,64]{2,1,0:T(8,128)S(1)} fusion(bf16[7,64,1024]{2,1,0:T(8,128)(2,1)} %param.10, bf16[16,1024]{1,0:T(8,128)(2,1)} %param.6, pred[1024]{0:T(1024)(128)(4,1)S(1)} %iota_compare_fusion.2), kind=kOutput, calls=%fused_computation.8 | convolution fusion | flops 14696448 | bytes 979968 | tf_op jit(solution)/shard_map/pm,krm->kpr/dot_general | solution.py:38
  3.2 0.1 pad_maximum_fusion
  3.4 0.8 %fusion.21 = f32[16,1024]{1,0:T(8,128)S(1)} fusion(bf16[16,1024]{1,0:T(8,128)(2,1)} %param.6, pred[1024]{0:T(1024)(128)(4,1)S(1)} %iota_compare_fusion.2), kind=kLoop, calls=%fused_computation.28 | loop fusion | flops 32768 | bytes 99328 | tf_op jit(solution)/shard_map/convert_element_type | solution.py:61
  4.2 0.3 collective-permute-done
  4.6 1.3 %select_select_fusion = f32[64,8,128]{2,1,0:T(8,128)} fusion(f32[8,128]{1,0:T(8,128)S(1)} %get-tuple-element.17, f32[8,128]{1,0:T(8,128)S(1)} %get-tuple-element.18, f32[8,128]{1,0:T(8,128)S(1)} %get-tuple-element.19, f32[8,128]{1,0:T(8,128)S(1)} %get-tuple-element.20, f32[8,128]{1,0:T(8,128)S(1)} %get-tuple-element.21, f32[8,128]{1,0:T(8,128)S(1)} %get-tuple-element.16, ...), kind=kLoop, calls=%fused_computation.10 | loop fusion | flops 393216 | bytes 287104 | tf_op jit(solution)/shard_map/jit(_where)/select_n | solution.py:47
  5.9 11.6 %all-to-all-start = ((f32[64,8,128]{2,1,0:T(8,128)}), f32[64,8,128]{2,1,0:T(8,128)S(1)}, u32[]{:S(2)}, u32[]{:S(2)}) async-start(f32[64,8,128]{2,1,0:T(8,128)} %select_select_fusion), calls=%async_computation | async-start | bytes 524288 | tf_op jit(solution)/shard_map/all_to_all | solution.py:48
  17.6 10.8 %all-to-all-done = f32[64,8,128]{2,1,0:T(8,128)S(1)} async-done(((f32[64,8,128]{2,1,0:T(8,128)}), f32[64,8,128]{2,1,0:T(8,128)S(1)}, u32[]{:S(2)}, u32[]{:S(2)}) %all-to-all-start) | async-done | bytes 262176 | tf_op jit(solution)/shard_map/all_to_all | solution.py:48
  29.1 0.3 convolution_bitcast_fusion.1
  29.4 0.7 %fusion.5 = f32[16,1024]{1,0:T(8,128)S(1)} fusion(f32[16,1024]{1,0:T(8,128)S(1)} %convolution_bitcast_fusion.1, bf16[1,1024,1024]{2,1,0:T(8,128)(2,1)S(1)} %copy-done, pred[1024]{0:T(1024)(128)(4,1)S(1)} %iota_compare_fusion.2, bf16[16,1024]{1,0:T(8,128)(2,1)S(1)} %copy-done.2), kind=kOutput, calls=%fused_computation.3 | convolution fusion | flops 33603584 | bytes 2262016 | tf_op jit(solution)/shard_map/rc,pc->pr/dot_general | solution.py:41
  30.1 0.2 fusion.8
  30.2 0.3 fusion.9
  30.7 1.2 %collective-permute-done.1 = f32[8,128]{1,0:T(8,128)S(1)} collective-permute-done((f32[8,128]{1,0:T(8,128)S(1)}, f32[8,128]{1,0:T(8,128)S(1)}, u32[]{:S(2)}, u32[]{:S(2)}) %collective-permute-start.1) | collective-permute-done | bytes 4128 | tf_op jit(solution)/shard_map/ppermute | solution.py:71
  31.9 15.6 %all_to_all.10 = f32[64,8,128]{2,1,0:T(8,128)S(1)} all-to-all(f32[64,8,128]{2,1,0:T(8,128)S(1)} %broadcast_in_dim.137), channel_id=1, replica_groups=mesh['gx_0'=4,'gx_1'=4,'gy_0'=4,'gy_1'=2] {'gx_0','gx_1','gy_0'}, dimensions={0} | all-to-all | bytes 524288 | tf_op jit(solution)/shard_map/all_to_all | solution.py:73
  47.7 0.1 copy.18
  47.8 0.2 convolution_subtract_fusion
  47.9 0.1 fusion.28
  48.0 0.1 fusion.26
  48.3 0.1 convolution_add_fusion
  48.5 1.5 %cholesky.18 = f32[16,16]{1,0:T(8,128)S(1)} custom-call(f32[16,16]{1,0:T(8,128)S(1)} %fusion.33), custom_call_target="Cholesky" | custom-call | tf_op jit(solution)/shard_map/jit(cholesky)/cholesky | solution.py:79
  50.0 0.6 %compare_reduce_fusion = pred[]{:T(512)} fusion(f32[16]{0:T(128)S(1)} %select_reduce_fusion), kind=kLoop, calls=%fused_computation.95 | loop fusion | flops 31 | bytes 65 | tf_op jit(solution)/shard_map/jit(cholesky)/cholesky | solution.py:79
  50.6 1.2 %select_bitcast_fusion = (f32[1,16,16]{2,1,0:T(8,128)S(1)}, f32[16,16]{1,0:T(8,128)}) fusion(f32[16,16]{1,0:T(8,128)S(1)} %cholesky.18, pred[]{:T(512)} %compare_reduce_fusion), kind=kLoop, calls=%fused_computation.55 | loop fusion | flops 1024 | bytes 3073 | tf_op jit(solution)/shard_map/jit(_solve_triangular)/triangular_solve | solution.py:80
  51.9 1.2 %custom-call.7 = f32[1,16,16]{1,2,0:T(8,128)S(1)} custom-call(f32[1,16,16]{2,1,0:T(8,128)S(1)} %get-tuple-element.12), custom_call_target="InvertDiagBlocksLowerTriangular" | custom-call | tf_op jit(solution)/shard_map/jit(_solve_triangular)/triangular_solve | solution.py:80
  53.1 0.7 %copy.22 = f32[16,16]{1,0:T(8,128)} copy(f32[16,16]{0,1:T(8,128)S(1)} %split.16) | data formatting | bytes 2048
  53.8 0.9 %fusion.31 = f32[16,1024]{1,0:T(8,128)} fusion(f32[16,1024]{1,0:T(8,128)S(1)} %convolution_subtract_fusion, f32[1,16,16]{1,2,0:T(8,128)S(1)} %custom-call.7), kind=kOutput, calls=%fused_computation.51 | convolution fusion | flops 3145728 | bytes 132096 | tf_op jit(solution)/shard_map/jit(_solve_triangular)/triangular_solve | solution.py:80
  (60 shorter events, 1.5 us)
Async XLA Ops:
  0.6 28.8 %copy-start = (bf16[1,1024,1024]{2,1,0:T(8,128)(2,1)S(1)}, bf16[1,1024,1024]{2,1,0:T(8,128)(2,1)}, u32[]{:S(2)}) copy-start(bf16[1,1024,1024]{2,1,0:T(8,128)(2,1)} %param.9) | copy-start | bytes 6291460
  0.6 28.5 %copy-start.1 = (bf16[7,64,1024]{2,1,0:T(8,128)(2,1)S(1)}, bf16[7,64,1024]{2,1,0:T(8,128)(2,1)}, u32[]{:S(2)}) copy-start(bf16[7,64,1024]{2,1,0:T(8,128)(2,1)} %param.10) | copy-start | bytes 2752516
  0.7 28.7 %copy-start.2 = (bf16[16,1024]{1,0:T(8,128)(2,1)S(1)}, bf16[16,1024]{1,0:T(8,128)(2,1)}, u32[]{:S(2)}) copy-start(bf16[16,1024]{1,0:T(8,128)(2,1)} %param.6) | copy-start | bytes 98308
  3.3 1.2 %collective-permute-start = (f32[7,8,128]{2,1,0:T(8,128)S(1)}, f32[7,8,128]{2,1,0:T(8,128)S(1)}, u32[]{:S(2)}, u32[]{:S(2)}) collective-permute-start(f32[7,8,128]{2,1,0:T(8,128)S(1)} %pad_maximum_fusion), channel_id=1, source_target_pairs={{0,1},{1,0},{2,3},{3,2},{4,5},{5,4},{6,7},{7,6},{8,9},{9,8},{10,11... | collective-permute-start | bytes 86024 | tf_op jit(solution)/shard_map/ppermute | solution.py:40
  5.9 24.2 %copy-start.3 = (bf16[16,1024]{1,0:T(8,128)(2,1)S(1)}, bf16[16,1024]{1,0:T(8,128)(2,1)}, u32[]{:S(2)}) copy-start(bf16[16,1024]{1,0:T(8,128)(2,1)} %param.7) | copy-start | bytes 98308
  5.9 24.2 %copy-start.4 = (f32[16,16]{1,0:T(8,128)S(1)}, f32[16,16]{1,0:T(8,128)}, u32[]{:S(2)}) copy-start(f32[16,16]{1,0:T(8,128)} %param.8) | copy-start | bytes 3076
  5.9 22.6 %all-to-all-start = ((f32[64,8,128]{2,1,0:T(8,128)}), f32[64,8,128]{2,1,0:T(8,128)S(1)}, u32[]{:S(2)}, u32[]{:S(2)}) async-start(f32[64,8,128]{2,1,0:T(8,128)} %select_select_fusion), calls=%async_computation | async-start | bytes 524288 | tf_op jit(solution)/shard_map/all_to_all | solution.py:48
  30.7 1.2 %collective-permute-start.1 = (f32[8,128]{1,0:T(8,128)S(1)}, f32[8,128]{1,0:T(8,128)S(1)}, u32[]{:S(2)}, u32[]{:S(2)}) collective-permute-start(f32[8,128]{1,0:T(8,128)S(1)} %fusion.35), channel_id=1, source_target_pairs={{0,1},{1,0},{2,3},{3,2},{4,5},{5,4},{6,7},{7,6},{8,9},{9,8},{10,11... | collective-permute-start | bytes 12296 | tf_op jit(solution)/shard_map/ppermute | solution.py:71

commit v2 on v1

v2 whole, which is shorter than its diff:
```python
import functools
import math

import jax
import jax.numpy as jnp
from jax import lax
from jax.experimental import pallas as pl
from jax.experimental.pallas import tpu as pltpu
from jax.sharding import Mesh
from jax.sharding import PartitionSpec as P

AXES = ("gx_0", "gx_1", "gy_0", "gy_1")
CHIPS = ("gx_0", "gx_1", "gy_0")
CORE = "gy_1"
HIGHEST = lax.Precision.HIGHEST
VMEM = pl.BlockSpec(memory_space=pltpu.VMEM)
SMEM = pl.BlockSpec(memory_space=pltpu.SMEM)
HBM = pl.BlockSpec(memory_space=pltpu.HBM)
LIMIT = 32 * 1024 * 1024
FIRST_LIMIT = 55200 * 1024
F32 = jnp.float32
LANES = 128


def fold(m):
    half = m.shape[-2] // 2
    return jnp.concatenate([m[..., :half, :], m[..., half:, :]], -1)


def unfold(m):
    half = m.shape[-1] // 2
    return jnp.concatenate([m[..., :half], m[..., half:]], -2)


def contract(a, b, over, precision=None):
    return lax.dot_general(
        a, b, ((over[:1], over[1:]), ((), ())), precision=precision, preferred_element_type=F32
    )


def call(kernel, outs, ins, scratch=(), flops=0, moved=0, limit=LIMIT):
    return pl.pallas_call(
        kernel,
        out_shape=outs,
        in_specs=ins,
        out_specs=jax.tree.map(lambda _: VMEM, outs),
        scratch_shapes=list(scratch),
        compiler_params=pltpu.CompilerParams(vmem_limit_bytes=limit),
        cost_estimate=pl.CostEstimate(flops=flops, bytes_accessed=moved, transcendentals=0),
    )


def masked(sizes, raw):
    slot = lax.broadcasted_iota(jnp.int32, raw.shape, 1)
    return jnp.where(slot < sizes[0], raw.astype(F32), 0.0)


def coefficients(sizes, probes_hbm, bases_hbm, out_ref, probes, bases, sems):
    levels, rank, rows = bases.shape
    copies = [
        pltpu.make_async_copy(probes_hbm, probes, sems.at[0]),
        pltpu.make_async_copy(bases_hbm, bases, sems.at[1]),
    ]
    for copy in copies:
        copy.start()
    for copy in copies:
        copy.wait()
    block = masked(sizes, probes[...]).astype(probes.dtype)
    both = contract(block, bases[...].reshape(levels * rank, rows), (1, 1))
    for t in range(levels):
        out_ref[t] = fold(both[:, t * rank : (t + 1) * rank])


def chip_index():
    index = 0
    for axis in CHIPS:
        index = index * lax.axis_size(axis) + lax.axis_index(axis)
    return index


def outgoing(chip_bits, chip_ref, own, other, out_ref):
    chip = chip_ref[0]
    out_ref[chip] = jnp.zeros(own.shape[1:], F32)
    for bit in range(chip_bits):
        first = ((chip >> bit) ^ 1) << bit
        mine = own[bit + 1] + other[bit + 1]
        out_ref[pl.ds(first, 1 << bit)] = jnp.broadcast_to(mine[None], (1 << bit,) + mine.shape)


def coupled(chip_bits, chip_ref, sizes, got, other, bases, image, pull, block, shifted_ref, sums_ref):
    levels, rank, rows = bases.shape
    dense = block[...].astype(F32)
    chip = chip_ref[0]
    partners = [other[0]]
    for bit in range(chip_bits):
        first = ((chip >> bit) ^ 1) << bit
        partners.append(jnp.sum(got[pl.ds(first, 1 << bit)], axis=0))
    scaled = [
        unfold(partners[t] * (1.0 / math.sqrt(rank * rows * 2**t))) for t in range(levels)
    ]
    weights = jnp.concatenate(scaled, 1).astype(bases.dtype)
    far = contract(weights, bases[...].reshape(levels * rank, rows), (1, 0))
    full = masked(sizes, image[...] + far)
    shifted = full - pull[...]
    shifted_ref[...] = shifted
    corner = contract(shifted, shifted, (1, 1), HIGHEST)
    lower = contract(dense, jnp.concatenate([shifted, dense, full], 0), (1, 1), HIGHEST)
    sums_ref[...] = fold(jnp.concatenate([lower, corner], 1))


def last_part(inverse, got, shifted, block, rayleigh_ref, factor_ref, next_ref):
    total = unfold(jnp.sum(got[...], axis=0)) * inverse
    p = total.shape[0]
    block_shifted = total[:, :p]
    block_block = total[:, p : 2 * p]
    rayleigh = total[:, 2 * p : 3 * p]
    corner = total[:, 3 * p :]
    rayleigh_ref[...] = rayleigh
    right = contract(block_block, rayleigh, (1, 0), HIGHEST) - block_shifted
    gram = corner + contract(
        jnp.concatenate([rayleigh, -block_shifted], 0),
        jnp.concatenate([right, rayleigh], 0),
        (0, 0),
        HIGHEST,
    )
    residual = shifted[...] - contract(rayleigh, block[...].astype(F32), (0, 0), HIGHEST)
    starts = range(0, residual.shape[1], LANES)
    parts = [residual[:, at : at + LANES] for at in starts]
    row = lax.broadcasted_iota(jnp.int32, (p, LANES), 0)
    lane = lax.broadcasted_iota(jnp.int32, (p, LANES), 1)
    columns = [jnp.broadcast_to(gram[:, k : k + 1], (p, LANES)) for k in range(p)]
    factor = jnp.zeros((p, LANES), F32)
    scale = jnp.zeros((p, LANES), F32)
    for k in range(p):
        pivot = jnp.broadcast_to(columns[k][k : k + 1, :], (p, LANES))
        root = lax.rsqrt(pivot)
        ratio = jnp.where(row > k, columns[k], 0.0) * (1.0 / pivot)
        factor = jnp.where(lane == k, jnp.where(row >= k, columns[k], 0.0) * root, factor)
        scale = jnp.where(row == k, root, scale)
        for j in range(k + 1, p):
            columns[j] = columns[j] - ratio * columns[j][k : k + 1, :]
        parts = [part - ratio * part[k : k + 1, :] for part in parts]
    factor_ref[...] = factor[:, :p]
    for at, part in zip(starts, parts):
        next_ref[:, at : at + LANES] = part * scale


def body(probes, previous, prev_coupling, leaves, bases, leaf_sizes):
    probe_count = probes.shape[0]
    levels, rank, rows = bases.shape
    chips = lax.axis_size(CHIPS)
    chip_bits = chips.bit_length() - 1
    devices = lax.axis_size(AXES)
    inverse = 1.0 / (devices * rows * 3 // 4)
    chip = chip_index().astype(jnp.int32).reshape(1)
    swap = [(0, 1), (1, 0)]
    tile = (probe_count // 2, 2 * rank)
    wide = jax.ShapeDtypeStruct((probe_count, rows), F32)
    square = jax.ShapeDtypeStruct((probe_count, probe_count), F32)
    partials = call(
        coefficients,
        jax.ShapeDtypeStruct((levels,) + tile, F32),
        [SMEM, HBM, HBM],
        [
            pltpu.VMEM(probes.shape, probes.dtype),
            pltpu.VMEM(bases.shape, bases.dtype),
            pltpu.SemaphoreType.DMA((2,)),
        ],
        limit=FIRST_LIMIT,
    )(leaf_sizes, probes, bases)
    other = lax.ppermute(partials, CORE, swap)
    valid = (jnp.arange(rows, dtype=jnp.int32) < leaf_sizes[0])[None, :]
    block = jnp.where(valid, probes, jnp.zeros_like(probes))
    older = jnp.where(valid, previous, jnp.zeros_like(previous)).astype(F32)
    image = contract(block, leaves[0], (1, 0))
    pull = contract(prev_coupling, older, (1, 0), HIGHEST)
    other, image, pull, block = lax.optimization_barrier((other, image, pull, block))
    send = call(
        functools.partial(outgoing, chip_bits),
        jax.ShapeDtypeStruct((chips,) + tile, F32),
        [SMEM, VMEM, VMEM],
    )(chip, partials, other)
    got = lax.all_to_all(send, CHIPS, 0, 0, tiled=True)
    shifted, sums = call(
        functools.partial(coupled, chip_bits),
        (wide, jax.ShapeDtypeStruct((probe_count // 2, 8 * probe_count), F32)),
        [SMEM] * 2 + [VMEM] * 6,
    )(chip, leaf_sizes, got, other, bases, image, pull, block)
    sums = sums + lax.ppermute(sums, CORE, swap)
    spread = jnp.broadcast_to(sums[None], (chips,) + sums.shape)
    total = lax.all_to_all(spread, CHIPS, 0, 0, tiled=True)
    return call(
        functools.partial(last_part, inverse),
        (square, square, wide),
        [VMEM] * 3,
    )(total, shifted, block)


def solution(mesh):
    split = Mesh(mesh.devices.reshape(4, 4, 4, 2), AXES)
    return jax.shard_map(
        body,
        mesh=split,
        in_specs=(
            P(None, AXES),
            P(None, AXES),
            P(),
            P(AXES, None, None),
            P(None, None, AXES),
            P(AXES),
        ),
        out_specs=(P(), P(), P(None, AXES)),
        check_vma=False,
    )
```

time: 55 us -> 46.8 us (0.85)
  blocking collectives: 15.6 us -> 38.1 us
  starting transfers between devices: 11.7 us -> 0.09 us
  waiting for transfers between devices: 12.3 us -> 1.23 us
  other arithmetic: 7.29 us -> 0.78 us
  Pallas kernels: 0 us -> 4.13 us
  matrix products: 4.53 us -> 0.55 us
  local copies, waits for them, and re-layouts: 1.61 us -> 0.04 us
    all_to_all x1 -> x2, blocking collectives: 15.6 us -> 38.1 us  [the longest x1 22.5 us: body(): got = lax.all_to_all(send, CHIPS, 0, 0, tiled=True)]
    all_to_all x1 -> x0, starting transfers between devices: 11.6 us -> none  [body(): got = lax.all_to_all(send, CHIPS, 0, 0, tiled=True)]
    all_to_all x1 -> x0, waiting for transfers between devices: 10.8 us -> none  [body(): got = lax.all_to_all(send, CHIPS, 0, 0, tiled=True)]
    another operation x13 -> x0, other arithmetic: 4.67 us -> none  [the longest x2 2.47 us: body(): next_block = jax.scipy.linalg.solve_triangular(factor, residual, lower=True)]
    pallas_call x0 -> x4, Pallas kernels: none -> 4.13 us  [the longest x1 1.76 us: body(): call(coefficients, jax.ShapeDtypeStruct((levels,) + tile, F32), [SMEM, HB...]
    dot_general x9 -> x2, matrix products: 3.64 us -> 0.55 us  [contract(): lax.dot_general(a, b, ((over[:1], over[1:]), ((), ())), precision=precisi...]
    another operation x1 -> x0, matrix products: 0.88 us -> none  [body(): next_block = jax.scipy.linalg.solve_triangular(factor, residual, lower=True)]
    convert_element_type x1 -> x0, other arithmetic: 0.77 us -> none  [body(): dense = block.astype(jnp.float32)]
  transfers between devices with their start and end apart: 3 -> 2, of which waited for: 3 -> 1; matrix products, arithmetic and copies ran while one was open for 2% -> 3% of each run, Pallas kernels for 0% -> 0%
where the time goes in v2:
time: 46.8 us; the launch traced here: 46.5 us
  blocking collectives  38.1 us (81%)
  Pallas kernels  4.13 us (9%)
  between operations  1.52 us (3%)
  waiting for transfers between devices  1.23 us (3%)
  other arithmetic  0.78 us (2%)
  matrix products  0.55 us (1%)
    all_to_all x1, blocking collectives, body(): got = lax.all_to_all(send, CHIPS, 0, 0, tiled=True)  22.5 us
    all_to_all x1, blocking collectives, body(): total = lax.all_to_all(spread, CHIPS, 0, 0, tiled=True)  15.6 us
    pallas_call x1, Pallas kernels, body(): call(coefficients, jax.ShapeDtypeStruct((levels,) + tile, F32), [SMEM, HB...  1.76 us
    pallas_call x1, Pallas kernels, body(): call(functools.partial(last_part, inverse), (square, square, wide), [VMEM...  1.58 us
    ppermute x1, waiting for transfers between devices, body(): sums = sums + lax.ppermute(sums, CORE, swap)  1.23 us
  transfers between devices with their start and end apart: 2, of which 1 were waited for; matrix products, arithmetic and copies ran while one was open for 3% of the time, Pallas kernels for 0%

profile of v2, /device:TPU:0, one launch (start us, length us, event | category | flops | bytes accessed | tf_op | source)
XLA Modules:
  0.0 46.5 jit_solution(2735660466183921497)
XLA Ops:
  0.6 0.0 copy-start
  0.6 0.0 copy-start.3
  0.7 0.0 copy-start.2
  1.5 0.0 copy-start.1
  1.5 1.8 %shard_map.85.own = f32[7,8,128]{2,1,0:T(8,128)S(1)} custom-call(s32[1]{0:T(128)} %copy.9.sizes, bf16[16,1024]{1,0:T(8,128)(2,1)} %probes_hbm.1, bf16[7,64,1024]{2,1,0:T(8,128)(2,1)} %bases.1), custom_call_target="tpu_custom_call" | custom-call | tf_op jit(solution)/shard_map/pallas_call | solution.py:160
  3.2 0.1 collective-permute-start
  3.3 0.8 %broadcast_select_fusion.block = bf16[16,1024]{1,0:T(8,128)(2,1)S(1)} fusion(bf16[16,1024]{1,0:T(8,128)(2,1)} %probes_hbm.1, pred[1024]{0:T(1024)(128)(4,1)S(1)} %iota_compare_fusion), kind=kLoop, calls=%fused_computation.5 | loop fusion | flops 16384 | bytes 66560 | tf_op jit(solution)/shard_map/jit(_where)/select_n | solution.py:173
  4.1 0.0 copy-done
  4.1 0.4 fusion.image
  4.5 0.0 copy-done.3
  4.5 0.0 copy-done.2
  4.5 0.2 convolution_bitcast_fusion.pull
  4.7 0.0 collective-permute-done.other
  4.7 22.5 %all_to_all.10.got = f32[64,8,128]{2,1,0:T(8,128)S(1)} all-to-all(f32[64,8,128]{2,1,0:T(8,128)S(1)} %shard_map.86), channel_id=1, replica_groups=mesh['gx_0'=4,'gx_1'=4,'gy_0'=4,'gy_1'=2] {'gx_0','gx_1','gy_0'}, dimensions={0} | all-to-all | bytes 524288 | tf_op jit(solution)/shard_map/all_to_all | solution.py:183
  27.3 0.0 copy-done.1
  27.3 0.8 %shard_map.87 = (f32[16,1024]{1,0:T(8,128)S(1)}, f32[8,128]{1,0:T(8,128)S(1)}) custom-call(s32[1]{0:T(128)} %bitcast.chip_ref, s32[1]{0:T(128)} %copy.9.sizes, f32[64,8,128]{2,1,0:T(8,128)S(1)} %all_to_all.10.got, f32[7,8,128]{2,1,0:T(8,128)S(1)} %collective-permute-done.other, bf16[7,64,1024]{2,1,0:T(8,128)(2,1)S(1)} %copy-done.1, ...), custom_call_target="tpu_custom_call" | custom-call | tf_op jit(solution)/shard_map/pallas_call | solution.py:184
  28.0 0.0 collective-permute-start.1
  28.0 1.2 %collective-permute-done.1 = f32[8,128]{1,0:T(8,128)S(1)} collective-permute-done((f32[8,128]{1,0:T(8,128)S(1)}, f32[8,128]{1,0:T(8,128)S(1)}, u32[]{:S(2)}, u32[]{:S(2)}) %collective-permute-start.1) | collective-permute-done | bytes 4128 | tf_op jit(solution)/shard_map/ppermute | solution.py:189
  29.3 15.6 %all_to_all.11.got = f32[64,8,128]{2,1,0:T(8,128)S(1)} all-to-all(f32[64,8,128]{2,1,0:T(8,128)S(1)} %broadcast_in_dim.19), channel_id=1, replica_groups=mesh['gx_0'=4,'gx_1'=4,'gy_0'=4,'gy_1'=2] {'gx_0','gx_1','gy_0'}, dimensions={0} | all-to-all | bytes 524288 | tf_op jit(solution)/shard_map/all_to_all | solution.py:191
  44.9 1.6 %shard_map.88 = (f32[16,16]{1,0:T(8,128)}, f32[16,16]{1,0:T(8,128)}, f32[16,1024]{1,0:T(8,128)}) custom-call(f32[64,8,128]{2,1,0:T(8,128)S(1)} %all_to_all.11.got, f32[16,1024]{1,0:T(8,128)S(1)} %get-tuple-element.14.shifted, bf16[16,1024]{1,0:T(8,128)(2,1)S(1)} %broadcast_select_fusion.block), custom_call_target="tpu_custom_call" | custom-call | tf_op jit(solution)/shard_map/pallas_call | solution.py:192
  (4 shorter events, 0.1 us)
Async XLA Ops:
  0.6 3.5 %copy-start = (bf16[1,1024,1024]{2,1,0:T(8,128)(2,1)S(1)}, bf16[1,1024,1024]{2,1,0:T(8,128)(2,1)}, u32[]{:S(2)}) copy-start(bf16[1,1024,1024]{2,1,0:T(8,128)(2,1)} %param.9) | copy-start | bytes 6291460
  0.6 3.9 %copy-start.3 = (f32[16,16]{1,0:T(8,128)S(1)}, f32[16,16]{1,0:T(8,128)}, u32[]{:S(2)}) copy-start(f32[16,16]{1,0:T(8,128)} %param.8) | copy-start | bytes 3076
  0.7 3.8 %copy-start.2 = (bf16[16,1024]{1,0:T(8,128)(2,1)S(1)}, bf16[16,1024]{1,0:T(8,128)(2,1)}, u32[]{:S(2)}) copy-start(bf16[16,1024]{1,0:T(8,128)(2,1)} %param.7) | copy-start | bytes 98308
  1.5 25.8 %copy-start.1 = (bf16[7,64,1024]{2,1,0:T(8,128)(2,1)S(1)}, bf16[7,64,1024]{2,1,0:T(8,128)(2,1)}, u32[]{:S(2)}) copy-start(bf16[7,64,1024]{2,1,0:T(8,128)(2,1)} %bases.1) | copy-start | bytes 2752516
  3.2 1.5 %collective-permute-start = (f32[7,8,128]{2,1,0:T(8,128)S(1)}, f32[7,8,128]{2,1,0:T(8,128)S(1)}, u32[]{:S(2)}, u32[]{:S(2)}) collective-permute-start(f32[7,8,128]{2,1,0:T(8,128)S(1)} %shard_map.85.own), channel_id=1, source_target_pairs={{0,1},{1,0},{2,3},{3,2},{4,5},{5,4},{6,7},{7,6},{8,9},{9,8},{10,11... | collective-permute-start | bytes 86024 | tf_op jit(solution)/shard_map/ppermute | solution.py:171
  28.0 1.2 %collective-permute-start.1 = (f32[8,128]{1,0:T(8,128)S(1)}, f32[8,128]{1,0:T(8,128)S(1)}, u32[]{:S(2)}, u32[]{:S(2)}) collective-permute-start(f32[8,128]{1,0:T(8,128)S(1)} %get-tuple-element.13), channel_id=1, source_target_pairs={{0,1},{1,0},{2,3},{3,2},{4,5},{5,4},{6,7},{7,6},{8,9},{9,8},{10,11... | collective-permute-start | bytes 12296 | tf_op jit(solution)/shard_map/ppermute | solution.py:189

commit v3 on v2

--- a/solution.py
+++ b/solution.py
@@ -17,7 +17,7 @@
 SMEM = pl.BlockSpec(memory_space=pltpu.SMEM)
 HBM = pl.BlockSpec(memory_space=pltpu.HBM)
 LIMIT = 32 * 1024 * 1024
-FIRST_LIMIT = 55200 * 1024
+FIRST_LIMIT = 55150 * 1024
 F32 = jnp.float32
 LANES = 128
 
@@ -36,6 +36,19 @@
     return lax.dot_general(
         a, b, ((over[:1], over[1:]), ((), ())), precision=precision, preferred_element_type=F32
     )
+
+
+def split(x, dtype):
+    parts = []
+    for _ in range(3):
+        parts.append(x.astype(dtype))
+        x = x - parts[-1].astype(F32)
+    return parts
+
+
+def gather(x, size, axis):
+    parts = [lax.slice_in_dim(x, at, at + size, axis=axis) for at in (2 * size, size, 0)]
+    return parts[0] + parts[1] + parts[2]
 
 
 def call(kernel, outs, ins, scratch=(), flops=0, moved=0, limit=LIMIT):
@@ -55,7 +68,7 @@
     return jnp.where(slot < sizes[0], raw.astype(F32), 0.0)
 
 
-def coefficients(sizes, probes_hbm, bases_hbm, out_ref, probes, bases, sems):
+def coefficients(sizes, probes_hbm, bases_hbm, out_ref, block_ref, probes, bases, sems):
     levels, rank, rows = bases.shape
     copies = [
         pltpu.make_async_copy(probes_hbm, probes, sems.at[0]),
@@ -63,9 +76,10 @@
     ]
     for copy in copies:
         copy.start()
-    for copy in copies:
-        copy.wait()
+    copies[0].wait()
     block = masked(sizes, probes[...]).astype(probes.dtype)
+    block_ref[...] = block
+    copies[1].wait()
     both = contract(block, bases[...].reshape(levels * rank, rows), (1, 1))
     for t in range(levels):
         out_ref[t] = fold(both[:, t * rank : (t + 1) * rank])
@@ -89,7 +103,6 @@
 
 def coupled(chip_bits, chip_ref, sizes, got, other, bases, image, pull, block, shifted_ref, sums_ref):
     levels, rank, rows = bases.shape
-    dense = block[...].astype(F32)
     chip = chip_ref[0]
     partners = [other[0]]
     for bit in range(chip_bits):
@@ -103,9 +116,18 @@
     full = masked(sizes, image[...] + far)
     shifted = full - pull[...]
     shifted_ref[...] = shifted
-    corner = contract(shifted, shifted, (1, 1), HIGHEST)
-    lower = contract(dense, jnp.concatenate([shifted, dense, full], 0), (1, 1), HIGHEST)
-    sums_ref[...] = fold(jnp.concatenate([lower, corner], 1))
+    p = full.shape[0]
+    parts = split(shifted, bases.dtype) + [block[...]] + split(full, bases.dtype)
+    sums = contract(jnp.concatenate(parts[:4], 0), jnp.concatenate(parts, 0), (1, 1))
+    corner = gather(sums[: 3 * p, : 3 * p], p, 0)
+    lower = sums[3 * p :]
+    pieces = [
+        gather(lower[:, : 3 * p], p, 1),
+        lower[:, 3 * p : 4 * p],
+        gather(lower[:, 4 * p :], p, 1),
+        gather(corner, p, 1),
+    ]
+    sums_ref[...] = fold(jnp.concatenate(pieces, 1))
 
 
 def last_part(inverse, got, shifted, block, rayleigh_ref, factor_ref, next_ref):
@@ -157,9 +179,12 @@
     tile = (probe_count // 2, 2 * rank)
     wide = jax.ShapeDtypeStruct((probe_count, rows), F32)
     square = jax.ShapeDtypeStruct((probe_count, probe_count), F32)
-    partials = call(
+    partials, block = call(
         coefficients,
-        jax.ShapeDtypeStruct((levels,) + tile, F32),
+        (
+            jax.ShapeDtypeStruct((levels,) + tile, F32),
+            jax.ShapeDtypeStruct(probes.shape, probes.dtype),
+        ),
         [SMEM, HBM, HBM],
         [
             pltpu.VMEM(probes.shape, probes.dtype),
@@ -170,11 +195,10 @@
     )(leaf_sizes, probes, bases)
     other = lax.ppermute(partials, CORE, swap)
     valid = (jnp.arange(rows, dtype=jnp.int32) < leaf_sizes[0])[None, :]
-    block = jnp.where(valid, probes, jnp.zeros_like(probes))
     older = jnp.where(valid, previous, jnp.zeros_like(previous)).astype(F32)
     image = contract(block, leaves[0], (1, 0))
     pull = contract(prev_coupling, older, (1, 0), HIGHEST)
-    other, image, pull, block = lax.optimization_barrier((other, image, pull, block))
+    other, image, pull = lax.optimization_barrier((other, image, pull))
     send = call(
         functools.partial(outgoing, chip_bits),
         jax.ShapeDtypeStruct((chips,) + tile, F32),

time: 46.8 us -> 46.2 us (0.987)
  other arithmetic: 0.78 us -> 0.01 us
  waiting for transfers between devices: 1.23 us -> 1.79 us
    select_n x1 -> x0, other arithmetic: 0.77 us -> none  [body(): block = jnp.where(valid, probes, jnp.zeros_like(probes))]
    ppermute x1, waiting for transfers between devices: 0.01 us -> 0.6 us  [body(): other = lax.ppermute(partials, CORE, swap)]
  transfers between devices with their start and end apart: 2 -> 2, of which waited for: 1 -> 2; matrix products, arithmetic and copies ran while one was open for 3% -> 1% of each run, Pallas kernels for 0% -> 0%
where the time goes in v3:
time: 46.2 us; the launch traced here: 46 us
  blocking collectives  37.8 us (82%)
  Pallas kernels  4.15 us (9%)
  waiting for transfers between devices  1.79 us (4%)
  between operations  1.53 us (3%)
  matrix products  0.55 us (1%)
    all_to_all x1, blocking collectives, body(): got = lax.all_to_all(send, CHIPS, 0, 0, tiled=True)  22.2 us
    all_to_all x1, blocking collectives, body(): total = lax.all_to_all(spread, CHIPS, 0, 0, tiled=True)  15.6 us
    pallas_call x1, Pallas kernels, body(): call(coefficients, (jax.ShapeDtypeStruct((levels,) + tile, F32), jax.Shap...  1.79 us
    pallas_call x1, Pallas kernels, body(): call(functools.partial(last_part, inverse), (square, square, wide), [VMEM...  1.58 us
    ppermute x1, waiting for transfers between devices, body(): sums = sums + lax.ppermute(sums, CORE, swap)  1.2 us
  transfers between devices with their start and end apart: 2, of which 2 were waited for; matrix products, arithmetic and copies ran while one was open for 1% of the time, Pallas kernels for 0%

profile of v3, /device:TPU:0, one launch (start us, length us, event | category | flops | bytes accessed | tf_op | source)
XLA Modules:
  0.0 46.0 jit_solution(13740447171110467674)
XLA Ops:
  0.6 0.0 copy-start
  0.6 0.0 copy-start.1
  0.7 0.0 copy-start.3
  0.7 0.0 copy-start.2
  1.5 1.8 %shard_map.85 = (f32[7,8,128]{2,1,0:T(8,128)S(1)}, bf16[16,1024]{1,0:T(8,128)(2,1)S(1)}) custom-call(s32[1]{0:T(128)} %copy.9.sizes, bf16[16,1024]{1,0:T(8,128)(2,1)} %probes_hbm.1, bf16[7,64,1024]{2,1,0:T(8,128)(2,1)} %bases.1), custom_call_target="tpu_custom_call" | custom-call | tf_op jit(solution)/shard_map/pallas_call | solution.py:182
  3.3 0.1 collective-permute-start
  3.4 0.0 copy-done
  3.4 0.4 fusion.image
  3.8 0.0 copy-done.3
  3.8 0.0 copy-done.2
  3.8 0.2 convolution_bitcast_fusion.pull
  4.0 0.6 %collective-permute-done.other = f32[7,8,128]{2,1,0:T(8,128)S(1)} collective-permute-done((f32[7,8,128]{2,1,0:T(8,128)S(1)}, f32[7,8,128]{2,1,0:T(8,128)S(1)}, u32[]{:S(2)}, u32[]{:S(2)}) %collective-permute-start) | collective-permute-done | bytes 28704 | tf_op jit(solution)/shard_map/ppermute | solution.py:196
  4.6 22.2 %all_to_all.10.got = f32[64,8,128]{2,1,0:T(8,128)S(1)} all-to-all(f32[64,8,128]{2,1,0:T(8,128)S(1)} %shard_map.86), channel_id=1, replica_groups=mesh['gx_0'=4,'gx_1'=4,'gy_0'=4,'gy_1'=2] {'gx_0','gx_1','gy_0'}, dimensions={0} | all-to-all | bytes 524288 | tf_op jit(solution)/shard_map/all_to_all | solution.py:207
  26.8 0.0 copy-done.1
  26.8 0.8 %shard_map.87 = (f32[16,1024]{1,0:T(8,128)S(1)}, f32[8,128]{1,0:T(8,128)S(1)}) custom-call(s32[1]{0:T(128)} %bitcast.chip_ref, s32[1]{0:T(128)} %copy.9.sizes, f32[64,8,128]{2,1,0:T(8,128)S(1)} %all_to_all.10.got, f32[7,8,128]{2,1,0:T(8,128)S(1)} %collective-permute-done.other, bf16[7,64,1024]{2,1,0:T(8,128)(2,1)S(1)} %copy-done.1, ...), custom_call_target="tpu_custom_call" | custom-call | tf_op jit(solution)/shard_map/pallas_call | solution.py:208
  27.6 0.0 collective-permute-start.1
  27.6 1.2 %collective-permute-done.1 = f32[8,128]{1,0:T(8,128)S(1)} collective-permute-done((f32[8,128]{1,0:T(8,128)S(1)}, f32[8,128]{1,0:T(8,128)S(1)}, u32[]{:S(2)}, u32[]{:S(2)}) %collective-permute-start.1) | collective-permute-done | bytes 4128 | tf_op jit(solution)/shard_map/ppermute | solution.py:213
  28.8 15.6 %all_to_all.11.got = f32[64,8,128]{2,1,0:T(8,128)S(1)} all-to-all(f32[64,8,128]{2,1,0:T(8,128)S(1)} %broadcast_in_dim.20), channel_id=1, replica_groups=mesh['gx_0'=4,'gx_1'=4,'gy_0'=4,'gy_1'=2] {'gx_0','gx_1','gy_0'}, dimensions={0} | all-to-all | bytes 524288 | tf_op jit(solution)/shard_map/all_to_all | solution.py:215
  44.4 1.6 %shard_map.88 = (f32[16,16]{1,0:T(8,128)}, f32[16,16]{1,0:T(8,128)}, f32[16,1024]{1,0:T(8,128)}) custom-call(f32[64,8,128]{2,1,0:T(8,128)S(1)} %all_to_all.11.got, f32[16,1024]{1,0:T(8,128)S(1)} %get-tuple-element.16.shifted, bf16[16,1024]{1,0:T(8,128)(2,1)S(1)} %get-tuple-element.11.block), custom_call_target="tpu_custom_call" | custom-call | tf_op jit(solution)/shard_map/pallas_call | solution.py:216
  (4 shorter events, 0.1 us)
Async XLA Ops:
  0.6 2.7 %copy-start = (bf16[1,1024,1024]{2,1,0:T(8,128)(2,1)S(1)}, bf16[1,1024,1024]{2,1,0:T(8,128)(2,1)}, u32[]{:S(2)}) copy-start(bf16[1,1024,1024]{2,1,0:T(8,128)(2,1)} %param.9) | copy-start | bytes 6291460
  0.6 26.2 %copy-start.1 = (bf16[7,64,1024]{2,1,0:T(8,128)(2,1)S(1)}, bf16[7,64,1024]{2,1,0:T(8,128)(2,1)}, u32[]{:S(2)}) copy-start(bf16[7,64,1024]{2,1,0:T(8,128)(2,1)} %bases.1) | copy-start | bytes 2752516
  0.7 3.1 %copy-start.3 = (f32[16,16]{1,0:T(8,128)S(1)}, f32[16,16]{1,0:T(8,128)}, u32[]{:S(2)}) copy-start(f32[16,16]{1,0:T(8,128)} %param.8) | copy-start | bytes 3076
  0.7 3.1 %copy-start.2 = (bf16[16,1024]{1,0:T(8,128)(2,1)S(1)}, bf16[16,1024]{1,0:T(8,128)(2,1)}, u32[]{:S(2)}) copy-start(bf16[16,1024]{1,0:T(8,128)(2,1)} %param.7) | copy-start | bytes 98308
  3.3 1.3 %collective-permute-start = (f32[7,8,128]{2,1,0:T(8,128)S(1)}, f32[7,8,128]{2,1,0:T(8,128)S(1)}, u32[]{:S(2)}, u32[]{:S(2)}) collective-permute-start(f32[7,8,128]{2,1,0:T(8,128)S(1)} %get-tuple-element.10.own), channel_id=1, source_target_pairs={{0,1},{1,0},{2,3},{3,2},{4,5},{5,4},{6,7},{7,6},{8,9},{9,8},{10,11... | collective-permute-start | bytes 86024 | tf_op jit(solution)/shard_map/ppermute | solution.py:196
  27.6 1.2 %collective-permute-start.1 = (f32[8,128]{1,0:T(8,128)S(1)}, f32[8,128]{1,0:T(8,128)S(1)}, u32[]{:S(2)}, u32[]{:S(2)}) collective-permute-start(f32[8,128]{1,0:T(8,128)S(1)} %get-tuple-element.15), channel_id=1, source_target_pairs={{0,1},{1,0},{2,3},{3,2},{4,5},{5,4},{6,7},{7,6},{8,9},{9,8},{10,11... | collective-permute-start | bytes 12296 | tf_op jit(solution)/shard_map/ppermute | solution.py:213

commit v4 on v3

--- a/solution.py
+++ b/solution.py
@@ -68,18 +68,15 @@
     return jnp.where(slot < sizes[0], raw.astype(F32), 0.0)
 
 
-def coefficients(sizes, probes_hbm, bases_hbm, out_ref, block_ref, probes, bases, sems):
+def keep_mask(sizes, keep_ref):
+    slot = lax.broadcasted_iota(jnp.int32, keep_ref.shape, 1)
+    keep_ref[...] = jnp.where(slot < sizes[0], 1.0, 0.0)
+
+
+def coefficients(keep, probes, bases, out_ref, block_ref):
     levels, rank, rows = bases.shape
-    copies = [
-        pltpu.make_async_copy(probes_hbm, probes, sems.at[0]),
-        pltpu.make_async_copy(bases_hbm, bases, sems.at[1]),
-    ]
-    for copy in copies:
-        copy.start()
-    copies[0].wait()
-    block = masked(sizes, probes[...]).astype(probes.dtype)
+    block = jnp.where(keep[:1] > 0.0, probes[...].astype(F32), 0.0).astype(probes.dtype)
     block_ref[...] = block
-    copies[1].wait()
     both = contract(block, bases[...].reshape(levels * rank, rows), (1, 1))
     for t in range(levels):
         out_ref[t] = fold(both[:, t * rank : (t + 1) * rank])
@@ -113,8 +110,8 @@
     ]
     weights = jnp.concatenate(scaled, 1).astype(bases.dtype)
     far = contract(weights, bases[...].reshape(levels * rank, rows), (1, 0))
-    full = masked(sizes, image[...] + far)
-    shifted = full - pull[...]
+    full = image[...] + far
+    shifted = masked(sizes, full - pull[...])
     shifted_ref[...] = shifted
     p = full.shape[0]
     parts = split(shifted, bases.dtype) + [block[...]] + split(full, bases.dtype)
@@ -179,25 +176,26 @@
     tile = (probe_count // 2, 2 * rank)
     wide = jax.ShapeDtypeStruct((probe_count, rows), F32)
     square = jax.ShapeDtypeStruct((probe_count, probe_count), F32)
+    keep = call(
+        keep_mask,
+        jax.ShapeDtypeStruct((8, rows), F32),
+        [SMEM],
+        flops=1000000000,
+        moved=0,
+    )(leaf_sizes)
     partials, block = call(
         coefficients,
         (
             jax.ShapeDtypeStruct((levels,) + tile, F32),
             jax.ShapeDtypeStruct(probes.shape, probes.dtype),
         ),
-        [SMEM, HBM, HBM],
-        [
-            pltpu.VMEM(probes.shape, probes.dtype),
-            pltpu.VMEM(bases.shape, bases.dtype),
-            pltpu.SemaphoreType.DMA((2,)),
-        ],
-        limit=FIRST_LIMIT,
-    )(leaf_sizes, probes, bases)
+        [VMEM] * 3,
+        flops=2 * probe_count * levels * rank * rows,
+        moved=2 * levels * rank * rows,
+    )(keep, probes, bases)
     other = lax.ppermute(partials, CORE, swap)
-    valid = (jnp.arange(rows, dtype=jnp.int32) < leaf_sizes[0])[None, :]
-    older = jnp.where(valid, previous, jnp.zeros_like(previous)).astype(F32)
     image = contract(block, leaves[0], (1, 0))
-    pull = contract(prev_coupling, older, (1, 0), HIGHEST)
+    pull = contract(prev_coupling, previous.astype(F32), (1, 0), HIGHEST)
     other, image, pull = lax.optimization_barrier((other, image, pull))
     send = call(
         functools.partial(outgoing, chip_bits),

time: 46.2 us -> 45.3 us (0.981)
  Pallas kernels: 4.15 us -> 2.75 us
  local copies, waits for them, and re-layouts: 0.04 us -> 0.6 us
    pallas_call x1, Pallas kernels: 1.79 us -> 0.39 us  [body(): call(coefficients, (jax.ShapeDtypeStruct((levels,) + tile, F32), jax.Shap...]
    unnamed x8 -> x10, local copies, waits for them, and re-layouts: 0.02 us -> 0.58 us
where the time goes in v4:
time: 45.3 us; the launch traced here: 45.1 us
  blocking collectives  37.8 us (83%)
  Pallas kernels  2.75 us (6%)
  waiting for transfers between devices  1.77 us (4%)
  between operations  1.51 us (3%)
  local copies, waits for them, and re-layouts  0.6 us (1%)
  matrix products  0.55 us (1%)
    all_to_all x1, blocking collectives, body(): got = lax.all_to_all(send, CHIPS, 0, 0, tiled=True)  22.2 us
    all_to_all x1, blocking collectives, body(): total = lax.all_to_all(spread, CHIPS, 0, 0, tiled=True)  15.6 us
    pallas_call x1, Pallas kernels, body(): call(functools.partial(last_part, inverse), (square, square, wide), [VMEM...  1.58 us
    ppermute x1, waiting for transfers between devices, body(): sums = sums + lax.ppermute(sums, CORE, swap)  1.2 us
  transfers between devices with their start and end apart: 2, of which 2 were waited for; matrix products, arithmetic and copies ran while one was open for 1% of the time, Pallas kernels for 0%

profile of v4, /device:TPU:0, one launch (start us, length us, event | category | flops | bytes accessed | tf_op | source)
XLA Modules:
  0.0 45.1 jit_solution(7812002122206247458)
XLA Ops:
  0.6 0.0 copy-start
  0.6 0.0 copy-start.1
  0.7 0.0 copy-start.2
  1.5 0.5 %copy-done.1 = bf16[7,64,1024]{2,1,0:T(8,128)(2,1)S(1)} copy-done((bf16[7,64,1024]{2,1,0:T(8,128)(2,1)S(1)}, bf16[7,64,1024]{2,1,0:T(8,128)(2,1)}, u32[]{:S(2)}) %copy-start.1) | copy-done | bytes 917528
  2.0 0.0 copy-done.2
  2.0 0.0 copy-start.3
  2.0 0.0 copy-start.4
  2.0 0.4 shard_map.86
  2.4 0.1 collective-permute-start
  2.5 0.0 copy-done
  2.5 0.4 fusion.image
  2.9 0.0 copy-done.3
  2.9 0.0 copy-done.4
  2.9 0.2 fusion.2.pull
  3.1 0.6 %collective-permute-done.other = f32[7,8,128]{2,1,0:T(8,128)S(1)} collective-permute-done((f32[7,8,128]{2,1,0:T(8,128)S(1)}, f32[7,8,128]{2,1,0:T(8,128)S(1)}, u32[]{:S(2)}, u32[]{:S(2)}) %collective-permute-start) | collective-permute-done | bytes 28704 | tf_op jit(solution)/shard_map/ppermute | solution.py:196
  3.7 22.2 %all_to_all.10.got = f32[64,8,128]{2,1,0:T(8,128)S(1)} all-to-all(f32[64,8,128]{2,1,0:T(8,128)S(1)} %shard_map.87), channel_id=1, replica_groups=mesh['gx_0'=4,'gx_1'=4,'gy_0'=4,'gy_1'=2] {'gx_0','gx_1','gy_0'}, dimensions={0} | all-to-all | bytes 524288 | tf_op jit(solution)/shard_map/all_to_all | solution.py:205
  25.9 0.8 %shard_map.88 = (f32[16,1024]{1,0:T(8,128)S(1)}, f32[8,128]{1,0:T(8,128)S(1)}) custom-call(s32[1]{0:T(128)} %bitcast.chip_ref, s32[1]{0:T(128)S(6)} %copy.9.sizes, f32[64,8,128]{2,1,0:T(8,128)S(1)} %all_to_all.10.got, f32[7,8,128]{2,1,0:T(8,128)S(1)} %collective-permute-done.other, bf16[7,64,1024]{2,1,0:T(8,128)(2,1)S(1)} %copy-done.1, ...), custom_call_target="tpu_custom_call" | custom-call | tf_op jit(solution)/shard_map/pallas_call | solution.py:206
  26.7 0.0 collective-permute-start.1
  26.7 1.2 %collective-permute-done.1 = f32[8,128]{1,0:T(8,128)S(1)} collective-permute-done((f32[8,128]{1,0:T(8,128)S(1)}, f32[8,128]{1,0:T(8,128)S(1)}, u32[]{:S(2)}, u32[]{:S(2)}) %collective-permute-start.1) | collective-permute-done | bytes 4128 | tf_op jit(solution)/shard_map/ppermute | solution.py:211
  27.9 15.6 %all_to_all.11.got = f32[64,8,128]{2,1,0:T(8,128)S(1)} all-to-all(f32[64,8,128]{2,1,0:T(8,128)S(1)} %broadcast_in_dim.2), channel_id=1, replica_groups=mesh['gx_0'=4,'gx_1'=4,'gy_0'=4,'gy_1'=2] {'gx_0','gx_1','gy_0'}, dimensions={0} | all-to-all | bytes 524288 | tf_op jit(solution)/shard_map/all_to_all | solution.py:213
  43.5 1.6 %shard_map.89 = (f32[16,16]{1,0:T(8,128)}, f32[16,16]{1,0:T(8,128)}, f32[16,1024]{1,0:T(8,128)}) custom-call(f32[64,8,128]{2,1,0:T(8,128)S(1)} %all_to_all.11.got, f32[16,1024]{1,0:T(8,128)S(1)} %get-tuple-element.16.shifted, bf16[16,1024]{1,0:T(8,128)(2,1)S(1)} %get-tuple-element.11.block), custom_call_target="tpu_custom_call" | custom-call | tf_op jit(solution)/shard_map/pallas_call | solution.py:214
  (4 shorter events, 0.1 us)
Async XLA Ops:
  0.6 1.9 %copy-start = (bf16[1,1024,1024]{2,1,0:T(8,128)(2,1)S(1)}, bf16[1,1024,1024]{2,1,0:T(8,128)(2,1)}, u32[]{:S(2)}) copy-start(bf16[1,1024,1024]{2,1,0:T(8,128)(2,1)} %param.9) | copy-start | bytes 6291460
  0.6 1.3 %copy-start.1 = (bf16[7,64,1024]{2,1,0:T(8,128)(2,1)S(1)}, bf16[7,64,1024]{2,1,0:T(8,128)(2,1)}, u32[]{:S(2)}) copy-start(bf16[7,64,1024]{2,1,0:T(8,128)(2,1)} %bases.3) | copy-start | bytes 2752516
  0.7 1.3 %copy-start.2 = (bf16[16,1024]{1,0:T(8,128)(2,1)S(1)}, bf16[16,1024]{1,0:T(8,128)(2,1)}, u32[]{:S(2)}) copy-start(bf16[16,1024]{1,0:T(8,128)(2,1)} %probes.1) | copy-start | bytes 98308
  2.0 0.9 %copy-start.3 = (bf16[16,1024]{1,0:T(8,128)(2,1)S(1)}, bf16[16,1024]{1,0:T(8,128)(2,1)}, u32[]{:S(2)}) copy-start(bf16[16,1024]{1,0:T(8,128)(2,1)} %param.7) | copy-start | bytes 98308
  2.0 0.9 %copy-start.4 = (f32[16,16]{1,0:T(8,128)S(1)}, f32[16,16]{1,0:T(8,128)}, u32[]{:S(2)}) copy-start(f32[16,16]{1,0:T(8,128)} %param.8) | copy-start | bytes 3076
  2.4 1.3 %collective-permute-start = (f32[7,8,128]{2,1,0:T(8,128)S(1)}, f32[7,8,128]{2,1,0:T(8,128)S(1)}, u32[]{:S(2)}, u32[]{:S(2)}) collective-permute-start(f32[7,8,128]{2,1,0:T(8,128)S(1)} %get-tuple-element.10.own), channel_id=1, source_target_pairs={{0,1},{1,0},{2,3},{3,2},{4,5},{5,4},{6,7},{7,6},{8,9},{9,8},{10,11... | collective-permute-start | bytes 86024 | tf_op jit(solution)/shard_map/ppermute | solution.py:196
  26.7 1.2 %collective-permute-start.1 = (f32[8,128]{1,0:T(8,128)S(1)}, f32[8,128]{1,0:T(8,128)S(1)}, u32[]{:S(2)}, u32[]{:S(2)}) collective-permute-start(f32[8,128]{1,0:T(8,128)S(1)} %get-tuple-element.15), channel_id=1, source_target_pairs={{0,1},{1,0},{2,3},{3,2},{4,5},{5,4},{6,7},{7,6},{8,9},{9,8},{10,11... | collective-permute-start | bytes 12296 | tf_op jit(solution)/shard_map/ppermute | solution.py:211

commit v5 on v4

--- a/solution.py
+++ b/solution.py
@@ -15,9 +15,7 @@
 HIGHEST = lax.Precision.HIGHEST
 VMEM = pl.BlockSpec(memory_space=pltpu.VMEM)
 SMEM = pl.BlockSpec(memory_space=pltpu.SMEM)
-HBM = pl.BlockSpec(memory_space=pltpu.HBM)
 LIMIT = 32 * 1024 * 1024
-FIRST_LIMIT = 55150 * 1024
 F32 = jnp.float32
 LANES = 128
 
@@ -46,19 +44,14 @@
     return parts
 
 
-def gather(x, size, axis):
-    parts = [lax.slice_in_dim(x, at, at + size, axis=axis) for at in (2 * size, size, 0)]
-    return parts[0] + parts[1] + parts[2]
-
-
-def call(kernel, outs, ins, scratch=(), flops=0, moved=0, limit=LIMIT):
+def call(kernel, outs, ins, scratch=(), flops=0, moved=0):
     return pl.pallas_call(
         kernel,
         out_shape=outs,
         in_specs=ins,
         out_specs=jax.tree.map(lambda _: VMEM, outs),
         scratch_shapes=list(scratch),
-        compiler_params=pltpu.CompilerParams(vmem_limit_bytes=limit),
+        compiler_params=pltpu.CompilerParams(vmem_limit_bytes=LIMIT),
         cost_estimate=pl.CostEstimate(flops=flops, bytes_accessed=moved, transcendentals=0),
     )
 
@@ -82,6 +75,11 @@
         out_ref[t] = fold(both[:, t * rank : (t + 1) * rank])
 
 
+def own_part(block, leaf, previous, coupling, image_ref, pull_ref):
+    image_ref[...] = contract(block[...], leaf[0], (1, 0))
+    pull_ref[...] = contract(coupling[...], previous[...].astype(F32), (1, 0), HIGHEST)
+
+
 def chip_index():
     index = 0
     for axis in CHIPS:
@@ -105,26 +103,35 @@
     for bit in range(chip_bits):
         first = ((chip >> bit) ^ 1) << bit
         partners.append(jnp.sum(got[pl.ds(first, 1 << bit)], axis=0))
-    scaled = [
-        unfold(partners[t] * (1.0 / math.sqrt(rank * rows * 2**t))) for t in range(levels)
-    ]
-    weights = jnp.concatenate(scaled, 1).astype(bases.dtype)
+    tiles = [partners[t] * (1.0 / math.sqrt(rank * rows * 2**t)) for t in range(levels)]
+    low = lax.broadcasted_iota(jnp.int32, tiles[0].shape, 1) < rank
+    tiles += [jnp.zeros_like(tiles[0])] * (levels % 2)
+    turned = [pltpu.roll(tile, rank, 1) for tile in tiles]
+    pairs = range(0, levels, 2)
+    upper = jnp.concatenate([jnp.where(low, tiles[t], turned[t + 1]) for t in pairs], 1)
+    lower = jnp.concatenate([jnp.where(low, turned[t], tiles[t + 1]) for t in pairs], 1)
+    weights = jnp.concatenate([upper, lower], 0)[:, : levels * rank].astype(bases.dtype)
     far = contract(weights, bases[...].reshape(levels * rank, rows), (1, 0))
     full = image[...] + far
     shifted = masked(sizes, full - pull[...])
     shifted_ref[...] = shifted
     p = full.shape[0]
-    parts = split(shifted, bases.dtype) + [block[...]] + split(full, bases.dtype)
-    sums = contract(jnp.concatenate(parts[:4], 0), jnp.concatenate(parts, 0), (1, 1))
-    corner = gather(sums[: 3 * p, : 3 * p], p, 0)
-    lower = sums[3 * p :]
-    pieces = [
-        gather(lower[:, : 3 * p], p, 1),
-        lower[:, 3 * p : 4 * p],
-        gather(lower[:, 4 * p :], p, 1),
-        gather(corner, p, 1),
-    ]
-    sums_ref[...] = fold(jnp.concatenate(pieces, 1))
+    half = p // 2
+    shifted_parts = split(shifted, bases.dtype)
+    full_parts = split(full, bases.dtype)
+    left = jnp.concatenate([block[...]] + shifted_parts, 0)
+    sums = jnp.zeros((4 * p, LANES), F32)
+    for i in (2, 1, 0):
+        own = block[...] if i == 0 else jnp.zeros_like(block[...])
+        right = [shifted_parts[i], own, full_parts[i], shifted_parts[i]]
+        sums = sums + contract(left, jnp.concatenate(right + right, 0), (1, 1))
+    with_block = sums[:p]
+    with_shifted = (sums[3 * p :] + sums[2 * p : 3 * p]) + sums[p : 2 * p]
+    lane = lax.broadcasted_iota(jnp.int32, (half, LANES), 1)
+    side = LANES // 2
+    upper = jnp.where(lane < 3 * p, with_block[:half], with_shifted[:half])
+    lower = jnp.where(lane < side + 3 * p, with_block[half:], with_shifted[half:])
+    sums_ref[...] = jnp.where(lane < side, upper, lower)
 
 
 def last_part(inverse, got, shifted, block, rayleigh_ref, factor_ref, next_ref):
@@ -194,8 +201,13 @@
         moved=2 * levels * rank * rows,
     )(keep, probes, bases)
     other = lax.ppermute(partials, CORE, swap)
-    image = contract(block, leaves[0], (1, 0))
-    pull = contract(prev_coupling, previous.astype(F32), (1, 0), HIGHEST)
+    image, pull = call(
+        own_part,
+        (wide, wide),
+        [VMEM] * 4,
+        flops=2 * probe_count * rows * rows,
+        moved=2 * rows * rows,
+    )(block, leaves, previous, prev_coupling)
     other, image, pull = lax.optimization_barrier((other, image, pull))
     send = call(
         functools.partial(outgoing, chip_bits),

time: 45.3 us -> 45 us (level)
  waiting for transfers between devices: 1.77 us -> 1.2 us
  matrix products: 0.55 us -> 0 us
  local copies, waits for them, and re-layouts: 0.6 us -> 1.15 us
    ppermute x1, waiting for transfers between devices: 0.57 us -> 0.01 us  [body(): other = lax.ppermute(partials, CORE, swap)]
    unnamed x10, local copies, waits for them, and re-layouts: 0.58 us -> 1.13 us
    dot_general x2 -> x0, matrix products: 0.55 us -> none  [contract(): lax.dot_general(a, b, ((over[:1], over[1:]), ((), ())), precision=precisi...]
    pallas_call x0 -> x1, Pallas kernels: none -> 0.46 us  [body(): call(own_part, (wide, wide), [VMEM] * 4, flops=2 * probe_count * rows * r...]
  transfers between devices with their start and end apart: 2 -> 2, of which waited for: 2 -> 1; matrix products, arithmetic and copies ran while one was open for 1% -> 0% of each run, Pallas kernels for 0% -> 1%
where the time goes in v5:
time: 45 us; the launch traced here: 44.8 us
  blocking collectives  37.8 us (84%)
  Pallas kernels  3.14 us (7%)
  between operations  1.45 us (3%)
  waiting for transfers between devices  1.2 us (3%)
  local copies, waits for them, and re-layouts  1.15 us (3%)
    all_to_all x1, blocking collectives, body(): got = lax.all_to_all(send, CHIPS, 0, 0, tiled=True)  22.2 us
    all_to_all x1, blocking collectives, body(): total = lax.all_to_all(spread, CHIPS, 0, 0, tiled=True)  15.6 us
    pallas_call x1, Pallas kernels, body(): call(functools.partial(last_part, inverse), (square, square, wide), [VMEM...  1.58 us
    ppermute x1, waiting for transfers between devices, body(): sums = sums + lax.ppermute(sums, CORE, swap)  1.2 us
    unnamed x10, local copies, waits for them, and re-layouts  1.13 us
  transfers between devices with their start and end apart: 2, of which 1 were waited for; matrix products, arithmetic and copies ran while one was open for 0% of the time, Pallas kernels for 1%

profile of v5, /device:TPU:0, one launch (start us, length us, event | category | flops | bytes accessed | tf_op | source)
XLA Modules:
  0.0 44.8 jit_solution(17395353736664399676)
XLA Ops:
  0.6 0.0 copy-start
  0.6 0.0 copy-start.3
  1.4 0.0 copy-start.1
  1.4 0.0 copy-start.2
  1.4 0.0 copy-start.4
  1.4 0.4 copy-done
  1.8 0.0 copy-done.3
  1.8 0.4 shard_map.86
  2.2 0.1 collective-permute-start
  2.3 0.7 %copy-done.1 = bf16[1,1024,1024]{2,1,0:T(8,128)(2,1)S(1)} copy-done((bf16[1,1024,1024]{2,1,0:T(8,128)(2,1)S(1)}, bf16[1,1024,1024]{2,1,0:T(8,128)(2,1)}, u32[]{:S(2)}) %copy-start.1) | copy-done | bytes 2097176
  3.0 0.0 copy-done.2
  3.0 0.0 copy-done.4
  3.0 0.5 %shard_map.87 = (f32[16,1024]{1,0:T(8,128)S(1)}, f32[16,1024]{1,0:T(8,128)S(1)}) custom-call(bf16[16,1024]{1,0:T(8,128)(2,1)S(1)} %get-tuple-element.13.block, bf16[1,1024,1024]{2,1,0:T(8,128)(2,1)S(1)} %copy-done.1, bf16[16,1024]{1,0:T(8,128)(2,1)S(1)} %copy-done.2, f32[16,16]{1,0:T(8,128)S(1)} %copy-done.4), custom_call_target="tpu_custom_call" | custom-call | flops 33554432 | bytes 2097152 | tf_op jit(solution)/shard_map/pallas_call | solution.py:204
  3.5 0.0 collective-permute-done.other
  3.6 22.2 %all_to_all.10.got = f32[64,8,128]{2,1,0:T(8,128)S(1)} all-to-all(f32[64,8,128]{2,1,0:T(8,128)S(1)} %shard_map.88), channel_id=1, replica_groups=mesh['gx_0'=4,'gx_1'=4,'gy_0'=4,'gy_1'=2] {'gx_0','gx_1','gy_0'}, dimensions={0} | all-to-all | bytes 524288 | tf_op jit(solution)/shard_map/all_to_all | solution.py:217
  25.8 0.7 %shard_map.89 = (f32[16,1024]{1,0:T(8,128)S(1)}, f32[8,128]{1,0:T(8,128)S(1)}) custom-call(s32[1]{0:T(128)} %bitcast.chip_ref, s32[1]{0:T(128)S(6)} %copy.9.sizes, f32[64,8,128]{2,1,0:T(8,128)S(1)} %all_to_all.10.got, f32[7,8,128]{2,1,0:T(8,128)S(1)} %collective-permute-done.other, bf16[7,64,1024]{2,1,0:T(8,128)(2,1)S(1)} %copy-done, ...), custom_call_target="tpu_custom_call" | custom-call | tf_op jit(solution)/shard_map/pallas_call | solution.py:218
  26.4 0.0 collective-permute-start.1
  26.4 1.2 %collective-permute-done.1 = f32[8,128]{1,0:T(8,128)S(1)} collective-permute-done((f32[8,128]{1,0:T(8,128)S(1)}, f32[8,128]{1,0:T(8,128)S(1)}, u32[]{:S(2)}, u32[]{:S(2)}) %collective-permute-start.1) | collective-permute-done | bytes 4128 | tf_op jit(solution)/shard_map/ppermute | solution.py:223
  27.6 15.6 %all_to_all.11.got = f32[64,8,128]{2,1,0:T(8,128)S(1)} all-to-all(f32[64,8,128]{2,1,0:T(8,128)S(1)} %broadcast_in_dim.2), channel_id=1, replica_groups=mesh['gx_0'=4,'gx_1'=4,'gy_0'=4,'gy_1'=2] {'gx_0','gx_1','gy_0'}, dimensions={0} | all-to-all | bytes 524288 | tf_op jit(solution)/shard_map/all_to_all | solution.py:225
  43.2 1.6 %shard_map.90 = (f32[16,16]{1,0:T(8,128)}, f32[16,16]{1,0:T(8,128)}, f32[16,1024]{1,0:T(8,128)}) custom-call(f32[64,8,128]{2,1,0:T(8,128)S(1)} %all_to_all.11.got, f32[16,1024]{1,0:T(8,128)S(1)} %get-tuple-element.20.shifted, bf16[16,1024]{1,0:T(8,128)(2,1)S(1)} %get-tuple-element.13.block), custom_call_target="tpu_custom_call" | custom-call | tf_op jit(solution)/shard_map/pallas_call | solution.py:226
  (4 shorter events, 0.1 us)
Async XLA Ops:
  0.6 1.2 %copy-start = (bf16[7,64,1024]{2,1,0:T(8,128)(2,1)S(1)}, bf16[7,64,1024]{2,1,0:T(8,128)(2,1)}, u32[]{:S(2)}) copy-start(bf16[7,64,1024]{2,1,0:T(8,128)(2,1)} %bases.3) | copy-start | bytes 2752516
  0.6 1.2 %copy-start.3 = (bf16[16,1024]{1,0:T(8,128)(2,1)S(1)}, bf16[16,1024]{1,0:T(8,128)(2,1)}, u32[]{:S(2)}) copy-start(bf16[16,1024]{1,0:T(8,128)(2,1)} %probes.1) | copy-start | bytes 98308
  1.4 1.7 %copy-start.1 = (bf16[1,1024,1024]{2,1,0:T(8,128)(2,1)S(1)}, bf16[1,1024,1024]{2,1,0:T(8,128)(2,1)}, u32[]{:S(2)}) copy-start(bf16[1,1024,1024]{2,1,0:T(8,128)(2,1)} %leaf.1) | copy-start | bytes 6291460
  1.4 1.7 %copy-start.2 = (bf16[16,1024]{1,0:T(8,128)(2,1)S(1)}, bf16[16,1024]{1,0:T(8,128)(2,1)}, u32[]{:S(2)}) copy-start(bf16[16,1024]{1,0:T(8,128)(2,1)} %previous.1) | copy-start | bytes 98308
  1.4 1.6 %copy-start.4 = (f32[16,16]{1,0:T(8,128)S(1)}, f32[16,16]{1,0:T(8,128)}, u32[]{:S(2)}) copy-start(f32[16,16]{1,0:T(8,128)} %coupling.1) | copy-start | bytes 3076
  2.2 1.3 %collective-permute-start = (f32[7,8,128]{2,1,0:T(8,128)S(1)}, f32[7,8,128]{2,1,0:T(8,128)S(1)}, u32[]{:S(2)}, u32[]{:S(2)}) collective-permute-start(f32[7,8,128]{2,1,0:T(8,128)S(1)} %get-tuple-element.12.own), channel_id=1, source_target_pairs={{0,1},{1,0},{2,3},{3,2},{4,5},{5,4},{6,7},{7,6},{8,9},{9,8},{10,11... | collective-permute-start | bytes 86024 | tf_op jit(solution)/shard_map/ppermute | solution.py:203
  26.4 1.2 %collective-permute-start.1 = (f32[8,128]{1,0:T(8,128)S(1)}, f32[8,128]{1,0:T(8,128)S(1)}, u32[]{:S(2)}, u32[]{:S(2)}) collective-permute-start(f32[8,128]{1,0:T(8,128)S(1)} %get-tuple-element.19), channel_id=1, source_target_pairs={{0,1},{1,0},{2,3},{3,2},{4,5},{5,4},{6,7},{7,6},{8,9},{9,8},{10,11... | collective-permute-start | bytes 12296 | tf_op jit(solution)/shard_map/ppermute | solution.py:223

commit v6 on v5

--- a/solution.py
+++ b/solution.py
@@ -187,7 +187,7 @@
         keep_mask,
         jax.ShapeDtypeStruct((8, rows), F32),
         [SMEM],
-        flops=1000000000,
+        flops=700000000,
         moved=0,
     )(leaf_sizes)
     partials, block = call(

time: 45 us -> 45 us (level)
  local copies, waits for them, and re-layouts: 1.15 us -> 0.59 us
  waiting for transfers between devices: 1.2 us -> 1.69 us
    unnamed x10, local copies, waits for them, and re-layouts: 1.13 us -> 0.57 us
    ppermute x1, waiting for transfers between devices: 0.01 us -> 0.5 us  [body(): other = lax.ppermute(partials, CORE, swap)]
  transfers between devices with their start and end apart: 2 -> 2, of which waited for: 1 -> 2; matrix products, arithmetic and copies ran while one was open for 0% -> 0% of each run, Pallas kernels for 1% -> 1%
where the time goes in v6:
time: 45 us; the launch traced here: 44.8 us
  blocking collectives  37.8 us (84%)
  Pallas kernels  3.12 us (7%)
  waiting for transfers between devices  1.69 us (4%)
  between operations  1.52 us (3%)
  local copies, waits for them, and re-layouts  0.59 us (1%)
    all_to_all x1, blocking collectives, body(): got = lax.all_to_all(send, CHIPS, 0, 0, tiled=True)  22.2 us
    all_to_all x1, blocking collectives, body(): total = lax.all_to_all(spread, CHIPS, 0, 0, tiled=True)  15.6 us
    pallas_call x1, Pallas kernels, body(): call(functools.partial(last_part, inverse), (square, square, wide), [VMEM...  1.58 us
    ppermute x1, waiting for transfers between devices, body(): sums = sums + lax.ppermute(sums, CORE, swap)  1.2 us
  transfers between devices with their start and end apart: 2, of which 2 were waited for; matrix products, arithmetic and copies ran while one was open for 0% of the time, Pallas kernels for 1%

profile of v6, /device:TPU:0, one launch (start us, length us, event | category | flops | bytes accessed | tf_op | source)
XLA Modules:
  0.0 44.8 jit_solution(17313517371273213954)
XLA Ops:
  0.6 0.0 copy-start
  0.6 0.0 copy-start.3
  0.7 0.0 copy-start.1
  0.7 0.0 copy-start.4
  0.7 0.0 copy-start.2
  1.5 0.3 copy-done
  1.8 0.0 copy-done.3
  1.8 0.4 shard_map.86
  2.2 0.1 collective-permute-start
  2.3 0.2 copy-done.1
  2.6 0.0 copy-done.4
  2.6 0.0 copy-done.2
  2.6 0.5 %shard_map.87 = (f32[16,1024]{1,0:T(8,128)S(1)}, f32[16,1024]{1,0:T(8,128)S(1)}) custom-call(bf16[16,1024]{1,0:T(8,128)(2,1)S(1)} %get-tuple-element.13.block, bf16[1,1024,1024]{2,1,0:T(8,128)(2,1)S(1)} %copy-done.1, bf16[16,1024]{1,0:T(8,128)(2,1)S(1)} %copy-done.2, f32[16,16]{1,0:T(8,128)S(1)} %copy-done.4), custom_call_target="tpu_custom_call" | custom-call | flops 33554432 | bytes 2097152 | tf_op jit(solution)/shard_map/pallas_call | solution.py:204
  3.0 0.5 %collective-permute-done.other = f32[7,8,128]{2,1,0:T(8,128)S(1)} collective-permute-done((f32[7,8,128]{2,1,0:T(8,128)S(1)}, f32[7,8,128]{2,1,0:T(8,128)S(1)}, u32[]{:S(2)}, u32[]{:S(2)}) %collective-permute-start) | collective-permute-done | bytes 28704 | tf_op jit(solution)/shard_map/ppermute | solution.py:203
  3.5 22.2 %all_to_all.10.got = f32[64,8,128]{2,1,0:T(8,128)S(1)} all-to-all(f32[64,8,128]{2,1,0:T(8,128)S(1)} %shard_map.88), channel_id=1, replica_groups=mesh['gx_0'=4,'gx_1'=4,'gy_0'=4,'gy_1'=2] {'gx_0','gx_1','gy_0'}, dimensions={0} | all-to-all | bytes 524288 | tf_op jit(solution)/shard_map/all_to_all | solution.py:217
  25.8 0.7 %shard_map.89 = (f32[16,1024]{1,0:T(8,128)S(1)}, f32[8,128]{1,0:T(8,128)S(1)}) custom-call(s32[1]{0:T(128)} %bitcast.chip_ref, s32[1]{0:T(128)S(6)} %copy.9.sizes, f32[64,8,128]{2,1,0:T(8,128)S(1)} %all_to_all.10.got, f32[7,8,128]{2,1,0:T(8,128)S(1)} %collective-permute-done.other, bf16[7,64,1024]{2,1,0:T(8,128)(2,1)S(1)} %copy-done, ...), custom_call_target="tpu_custom_call" | custom-call | tf_op jit(solution)/shard_map/pallas_call | solution.py:218
  26.4 0.0 collective-permute-start.1
  26.4 1.2 %collective-permute-done.1 = f32[8,128]{1,0:T(8,128)S(1)} collective-permute-done((f32[8,128]{1,0:T(8,128)S(1)}, f32[8,128]{1,0:T(8,128)S(1)}, u32[]{:S(2)}, u32[]{:S(2)}) %collective-permute-start.1) | collective-permute-done | bytes 4128 | tf_op jit(solution)/shard_map/ppermute | solution.py:223
  27.6 15.6 %all_to_all.11.got = f32[64,8,128]{2,1,0:T(8,128)S(1)} all-to-all(f32[64,8,128]{2,1,0:T(8,128)S(1)} %broadcast_in_dim.2), channel_id=1, replica_groups=mesh['gx_0'=4,'gx_1'=4,'gy_0'=4,'gy_1'=2] {'gx_0','gx_1','gy_0'}, dimensions={0} | all-to-all | bytes 524288 | tf_op jit(solution)/shard_map/all_to_all | solution.py:225
  43.2 1.6 %shard_map.90 = (f32[16,16]{1,0:T(8,128)}, f32[16,16]{1,0:T(8,128)}, f32[16,1024]{1,0:T(8,128)}) custom-call(f32[64,8,128]{2,1,0:T(8,128)S(1)} %all_to_all.11.got, f32[16,1024]{1,0:T(8,128)S(1)} %get-tuple-element.20.shifted, bf16[16,1024]{1,0:T(8,128)(2,1)S(1)} %get-tuple-element.13.block), custom_call_target="tpu_custom_call" | custom-call | tf_op jit(solution)/shard_map/pallas_call | solution.py:226
  (4 shorter events, 0.1 us)
Async XLA Ops:
  0.6 1.2 %copy-start = (bf16[7,64,1024]{2,1,0:T(8,128)(2,1)S(1)}, bf16[7,64,1024]{2,1,0:T(8,128)(2,1)}, u32[]{:S(2)}) copy-start(bf16[7,64,1024]{2,1,0:T(8,128)(2,1)} %bases.3) | copy-start | bytes 2752516
  0.6 1.2 %copy-start.3 = (bf16[16,1024]{1,0:T(8,128)(2,1)S(1)}, bf16[16,1024]{1,0:T(8,128)(2,1)}, u32[]{:S(2)}) copy-start(bf16[16,1024]{1,0:T(8,128)(2,1)} %probes.1) | copy-start | bytes 98308
  0.7 1.9 %copy-start.1 = (bf16[1,1024,1024]{2,1,0:T(8,128)(2,1)S(1)}, bf16[1,1024,1024]{2,1,0:T(8,128)(2,1)}, u32[]{:S(2)}) copy-start(bf16[1,1024,1024]{2,1,0:T(8,128)(2,1)} %leaf.1) | copy-start | bytes 6291460
  0.7 1.9 %copy-start.4 = (f32[16,16]{1,0:T(8,128)S(1)}, f32[16,16]{1,0:T(8,128)}, u32[]{:S(2)}) copy-start(f32[16,16]{1,0:T(8,128)} %coupling.1) | copy-start | bytes 3076
  0.7 1.9 %copy-start.2 = (bf16[16,1024]{1,0:T(8,128)(2,1)S(1)}, bf16[16,1024]{1,0:T(8,128)(2,1)}, u32[]{:S(2)}) copy-start(bf16[16,1024]{1,0:T(8,128)(2,1)} %previous.1) | copy-start | bytes 98308
  2.2 1.3 %collective-permute-start = (f32[7,8,128]{2,1,0:T(8,128)S(1)}, f32[7,8,128]{2,1,0:T(8,128)S(1)}, u32[]{:S(2)}, u32[]{:S(2)}) collective-permute-start(f32[7,8,128]{2,1,0:T(8,128)S(1)} %get-tuple-element.12.own), channel_id=1, source_target_pairs={{0,1},{1,0},{2,3},{3,2},{4,5},{5,4},{6,7},{7,6},{8,9},{9,8},{10,11... | collective-permute-start | bytes 86024 | tf_op jit(solution)/shard_map/ppermute | solution.py:203
  26.4 1.2 %collective-permute-start.1 = (f32[8,128]{1,0:T(8,128)S(1)}, f32[8,128]{1,0:T(8,128)S(1)}, u32[]{:S(2)}, u32[]{:S(2)}) collective-permute-start(f32[8,128]{1,0:T(8,128)S(1)} %get-tuple-element.19), channel_id=1, source_target_pairs={{0,1},{1,0},{2,3},{3,2},{4,5},{5,4},{6,7},{7,6},{8,9},{9,8},{10,11... | collective-permute-start | bytes 12296 | tf_op jit(solution)/shard_map/ppermute | solution.py:223

commit v7 on v6

--- a/solution.py
+++ b/solution.py
@@ -134,6 +134,10 @@
     sums_ref[...] = jnp.where(lane < side, upper, lower)
 
 
+def spread_out(own, other, out_ref):
+    out_ref[...] = jnp.broadcast_to((own[...] + other[...])[None], out_ref.shape)
+
+
 def last_part(inverse, got, shifted, block, rayleigh_ref, factor_ref, next_ref):
     total = unfold(jnp.sum(got[...], axis=0)) * inverse
     p = total.shape[0]
@@ -150,25 +154,40 @@
         HIGHEST,
     )
     residual = shifted[...] - contract(rayleigh, block[...].astype(F32), (0, 0), HIGHEST)
+    half = p // 2
+    tops = (0, half)
     starts = range(0, residual.shape[1], LANES)
-    parts = [residual[:, at : at + LANES] for at in starts]
-    row = lax.broadcasted_iota(jnp.int32, (p, LANES), 0)
-    lane = lax.broadcasted_iota(jnp.int32, (p, LANES), 1)
-    columns = [jnp.broadcast_to(gram[:, k : k + 1], (p, LANES)) for k in range(p)]
-    factor = jnp.zeros((p, LANES), F32)
-    scale = jnp.zeros((p, LANES), F32)
+    row = lax.broadcasted_iota(jnp.int32, (half, LANES), 0)
+    lane = lax.broadcasted_iota(jnp.int32, (half, LANES), 1)
+    columns = [
+        [jnp.broadcast_to(gram[top : top + half, k : k + 1], (half, LANES)) for k in range(p)]
+        for top in tops
+    ]
+    parts = [[residual[top : top + half, at : at + LANES] for at in starts] for top in tops]
+    factor = [jnp.zeros((half, LANES), F32) for _ in tops]
+    scale = [jnp.zeros((half, LANES), F32) for _ in tops]
     for k in range(p):
-        pivot = jnp.broadcast_to(columns[k][k : k + 1, :], (p, LANES))
+        side, at = divmod(k, half)
+        here = slice(at, at + 1)
+        pivot = jnp.broadcast_to(columns[side][k][here], (half, LANES))
         root = lax.rsqrt(pivot)
-        ratio = jnp.where(row > k, columns[k], 0.0) * (1.0 / pivot)
-        factor = jnp.where(lane == k, jnp.where(row >= k, columns[k], 0.0) * root, factor)
-        scale = jnp.where(row == k, root, scale)
-        for j in range(k + 1, p):
-            columns[j] = columns[j] - ratio * columns[j][k : k + 1, :]
-        parts = [part - ratio * part[k : k + 1, :] for part in parts]
-    factor_ref[...] = factor[:, :p]
-    for at, part in zip(starts, parts):
-        next_ref[:, at : at + LANES] = part * scale
+        reciprocal = 1.0 / pivot
+        scale[side] = jnp.where(row == at, root, scale[side])
+        for part in range(side, 2):
+            column, ratio = columns[part][k], columns[part][k] * reciprocal
+            if part == side:
+                column = jnp.where(row >= at, column, 0.0)
+                ratio = jnp.where(row > at, ratio, 0.0)
+            factor[part] = jnp.where(lane == k, column * root, factor[part])
+            if part == side and at == half - 1:
+                continue
+            for j in range(k + 1, p):
+                columns[part][j] = columns[part][j] - ratio * columns[side][j][here]
+            parts[part] = [x - ratio * y[here] for x, y in zip(parts[part], parts[side])]
+    for part, top in enumerate(tops):
+        factor_ref[top : top + half] = factor[part][:, :p]
+        for at, x in zip(starts, parts[part]):
+            next_ref[top : top + half, at : at + LANES] = x * scale[part]
 
 
 def body(probes, previous, prev_coupling, leaves, bases, leaf_sizes):
@@ -220,8 +239,11 @@
         (wide, jax.ShapeDtypeStruct((probe_count // 2, 8 * probe_count), F32)),
         [SMEM] * 2 + [VMEM] * 6,
     )(chip, leaf_sizes, got, other, bases, image, pull, block)
-    sums = sums + lax.ppermute(sums, CORE, swap)
-    spread = jnp.broadcast_to(sums[None], (chips,) + sums.shape)
+    spread = call(
+        spread_out,
+        jax.ShapeDtypeStruct((chips,) + sums.shape, F32),
+        [VMEM] * 2,
+    )(sums, lax.ppermute(sums, CORE, swap))
     total = lax.all_to_all(spread, CHIPS, 0, 0, tiled=True)
     return call(
         functools.partial(last_part, inverse),

time: 45 us -> 45 us (level)
  no operation moved by 1% of the time
where the time goes in v7:
time: 45 us; the launch traced here: 44.8 us
  blocking collectives  37.8 us (84%)
  Pallas kernels  3.11 us (7%)
  waiting for transfers between devices  1.69 us (4%)
  between operations  1.52 us (3%)
  local copies, waits for them, and re-layouts  0.57 us (1%)
    all_to_all x1, blocking collectives, body(): got = lax.all_to_all(send, CHIPS, 0, 0, tiled=True)  22.2 us
    all_to_all x1, blocking collectives, body(): total = lax.all_to_all(spread, CHIPS, 0, 0, tiled=True)  15.6 us
    pallas_call x1, Pallas kernels, body(): call(functools.partial(last_part, inverse), (square, square, wide), [VMEM...  1.56 us
    ppermute x1, waiting for transfers between devices, body(): lax.ppermute(sums, CORE, swap)  1.2 us
  transfers between devices with their start and end apart: 2, of which 2 were waited for; matrix products, arithmetic and copies ran while one was open for 0% of the time, Pallas kernels for 1%

profile of v7, /device:TPU:0, one launch (start us, length us, event | category | flops | bytes accessed | tf_op | source)
XLA Modules:
  0.0 44.8 jit_solution(6933507818878471784)
XLA Ops:
  0.6 0.0 copy-start
  0.6 0.0 copy-start.3
  0.7 0.0 copy-start.1
  0.7 0.0 copy-start.4
  0.7 0.0 copy-start.2
  1.5 0.3 copy-done
  1.8 0.0 copy-done.3
  1.8 0.4 shard_map.86
  2.2 0.1 collective-permute-start
  2.3 0.2 copy-done.1
  2.6 0.0 copy-done.4
  2.6 0.0 copy-done.2
  2.6 0.5 %shard_map.87 = (f32[16,1024]{1,0:T(8,128)S(1)}, f32[16,1024]{1,0:T(8,128)S(1)}) custom-call(bf16[16,1024]{1,0:T(8,128)(2,1)S(1)} %get-tuple-element.13.block, bf16[1,1024,1024]{2,1,0:T(8,128)(2,1)S(1)} %copy-done.1, bf16[16,1024]{1,0:T(8,128)(2,1)S(1)} %copy-done.2, f32[16,16]{1,0:T(8,128)S(1)} %copy-done.4), custom_call_target="tpu_custom_call" | custom-call | flops 33554432 | bytes 2097152 | tf_op jit(solution)/shard_map/pallas_call | solution.py:223
  3.0 0.5 %collective-permute-done.other = f32[7,8,128]{2,1,0:T(8,128)S(1)} collective-permute-done((f32[7,8,128]{2,1,0:T(8,128)S(1)}, f32[7,8,128]{2,1,0:T(8,128)S(1)}, u32[]{:S(2)}, u32[]{:S(2)}) %collective-permute-start) | collective-permute-done | bytes 28704 | tf_op jit(solution)/shard_map/ppermute | solution.py:222
  3.5 22.2 %all_to_all.10.got = f32[64,8,128]{2,1,0:T(8,128)S(1)} all-to-all(f32[64,8,128]{2,1,0:T(8,128)S(1)} %shard_map.88), channel_id=1, replica_groups=mesh['gx_0'=4,'gx_1'=4,'gy_0'=4,'gy_1'=2] {'gx_0','gx_1','gy_0'}, dimensions={0} | all-to-all | bytes 524288 | tf_op jit(solution)/shard_map/all_to_all | solution.py:236
  25.8 0.7 %shard_map.89 = (f32[16,1024]{1,0:T(8,128)S(1)}, f32[8,128]{1,0:T(8,128)S(1)}) custom-call(s32[1]{0:T(128)} %bitcast.chip_ref, s32[1]{0:T(128)S(6)} %copy.9.sizes, f32[64,8,128]{2,1,0:T(8,128)S(1)} %all_to_all.10.got, f32[7,8,128]{2,1,0:T(8,128)S(1)} %collective-permute-done.other, bf16[7,64,1024]{2,1,0:T(8,128)(2,1)S(1)} %copy-done, ...), custom_call_target="tpu_custom_call" | custom-call | tf_op jit(solution)/shard_map/pallas_call | solution.py:237
  26.4 0.0 collective-permute-start.1
  26.4 1.2 %collective-permute-done.1.other = f32[8,128]{1,0:T(8,128)S(1)} collective-permute-done((f32[8,128]{1,0:T(8,128)S(1)}, f32[8,128]{1,0:T(8,128)S(1)}, u32[]{:S(2)}, u32[]{:S(2)}) %collective-permute-start.1) | collective-permute-done | bytes 4128 | tf_op jit(solution)/shard_map/ppermute | solution.py:246
  27.6 15.6 %all_to_all.11.got = f32[64,8,128]{2,1,0:T(8,128)S(1)} all-to-all(f32[64,8,128]{2,1,0:T(8,128)S(1)} %shard_map.90), channel_id=1, replica_groups=mesh['gx_0'=4,'gx_1'=4,'gy_0'=4,'gy_1'=2] {'gx_0','gx_1','gy_0'}, dimensions={0} | all-to-all | bytes 524288 | tf_op jit(solution)/shard_map/all_to_all | solution.py:247
  43.2 1.6 %shard_map.91 = (f32[16,16]{1,0:T(8,128)}, f32[16,16]{1,0:T(8,128)}, f32[16,1024]{1,0:T(8,128)}) custom-call(f32[64,8,128]{2,1,0:T(8,128)S(1)} %all_to_all.11.got, f32[16,1024]{1,0:T(8,128)S(1)} %get-tuple-element.20.shifted, bf16[16,1024]{1,0:T(8,128)(2,1)S(1)} %get-tuple-element.13.block), custom_call_target="tpu_custom_call" | custom-call | tf_op jit(solution)/shard_map/pallas_call | solution.py:248
  (3 shorter events, 0.0 us)
Async XLA Ops:
  0.6 1.2 %copy-start = (bf16[7,64,1024]{2,1,0:T(8,128)(2,1)S(1)}, bf16[7,64,1024]{2,1,0:T(8,128)(2,1)}, u32[]{:S(2)}) copy-start(bf16[7,64,1024]{2,1,0:T(8,128)(2,1)} %bases.3) | copy-start | bytes 2752516
  0.6 1.2 %copy-start.3 = (bf16[16,1024]{1,0:T(8,128)(2,1)S(1)}, bf16[16,1024]{1,0:T(8,128)(2,1)}, u32[]{:S(2)}) copy-start(bf16[16,1024]{1,0:T(8,128)(2,1)} %probes.1) | copy-start | bytes 98308
  0.7 1.9 %copy-start.1 = (bf16[1,1024,1024]{2,1,0:T(8,128)(2,1)S(1)}, bf16[1,1024,1024]{2,1,0:T(8,128)(2,1)}, u32[]{:S(2)}) copy-start(bf16[1,1024,1024]{2,1,0:T(8,128)(2,1)} %leaf.1) | copy-start | bytes 6291460
  0.7 1.9 %copy-start.4 = (f32[16,16]{1,0:T(8,128)S(1)}, f32[16,16]{1,0:T(8,128)}, u32[]{:S(2)}) copy-start(f32[16,16]{1,0:T(8,128)} %coupling.1) | copy-start | bytes 3076
  0.7 1.9 %copy-start.2 = (bf16[16,1024]{1,0:T(8,128)(2,1)S(1)}, bf16[16,1024]{1,0:T(8,128)(2,1)}, u32[]{:S(2)}) copy-start(bf16[16,1024]{1,0:T(8,128)(2,1)} %previous.1) | copy-start | bytes 98308
  2.2 1.3 %collective-permute-start = (f32[7,8,128]{2,1,0:T(8,128)S(1)}, f32[7,8,128]{2,1,0:T(8,128)S(1)}, u32[]{:S(2)}, u32[]{:S(2)}) collective-permute-start(f32[7,8,128]{2,1,0:T(8,128)S(1)} %get-tuple-element.12.own), channel_id=1, source_target_pairs={{0,1},{1,0},{2,3},{3,2},{4,5},{5,4},{6,7},{7,6},{8,9},{9,8},{10,11... | collective-permute-start | bytes 86024 | tf_op jit(solution)/shard_map/ppermute | solution.py:222
  26.4 1.2 %collective-permute-start.1 = (f32[8,128]{1,0:T(8,128)S(1)}, f32[8,128]{1,0:T(8,128)S(1)}, u32[]{:S(2)}, u32[]{:S(2)}) collective-permute-start(f32[8,128]{1,0:T(8,128)S(1)} %get-tuple-element.19.own), channel_id=1, source_target_pairs={{0,1},{1,0},{2,3},{3,2},{4,5},{5,4},{6,7},{7,6},{8,9},{9,8},{10,11... | collective-permute-start | bytes 12296 | tf_op jit(solution)/shard_map/ppermute | solution.py:246
